TPU v7x, 32 devices: a whole 2x2x4 slice. The times are simulated.
32 devices in a mesh: row: 4 (over x, core), seq: 8 (over z, y).
Axes of the slice: x: 2, y: 2, z: 4, core: 2. Of those that a mesh axis runs over, the one named last changes fastest.
Arguments:
- hidden: bfloat16 [4, 8192, 768], P('row', 'seq'), may hold values from -6 to 6
- lengths: int32 [4, 4], P('row'), may hold values from 0 to 8192, as said below
- cotangent: bfloat16 [4, 8192, 768], P('row', 'seq'), may hold values from -6 to 6
- norm_gain: bfloat16 [768], P(('row', 'seq')), may hold values from 0.099609375 to 1.8984375
- in_proj: bfloat16 [768, 3352], P(('row', 'seq')), may hold values from -0.21875 to 0.21875
- conv_weight: bfloat16 [4, 1792], P(None, ('row', 'seq')), may hold values from -3 to 3
- conv_bias: bfloat16 [1792], P(('row', 'seq')), may hold values from -0.5 to 0.5
- a_log: float32 [24], replicated, may hold values from -7 to 1
- dt_bias: float32 [24], replicated, may hold values from -6 to -3
- skip_weight: float32 [24], replicated, may hold values from 0.5 to 1.5
- inner_gain: bfloat16 [1536], P(('row', 'seq')), may hold values from 0.099609375 to 1.8984375
- out_proj: bfloat16 [1536, 768], P(('row', 'seq')), may hold values from -0.15625 to 0.15625
Outputs:
- block_out: bfloat16 [4, 8192, 768], P('row', 'seq')
- hidden_grad: bfloat16 [4, 8192, 768], P('row', 'seq')
- norm_gain_grad: float32 [768], P(('row', 'seq'))
- in_proj_grad: float32 [768, 3352], P(('row', 'seq'))
- conv_weight_grad: float32 [4, 1792], P(None, ('row', 'seq'))
- conv_bias_grad: float32 [1792], P(('row', 'seq'))
- a_log_grad: float32 [24], replicated
- dt_bias_grad: float32 [24], replicated
- skip_d_grad: float32 [24], replicated
- inner_gain_grad: float32 [1536], P(('row', 'seq'))
- out_proj_grad: float32 [1536, 768], P(('row', 'seq'))
Inputs may be any that keep to these rules, and one draw needn't show every extreme that they name: Each row lists its sequences' lengths in order, each 2048 or more, and zeros only after the last sequence; a row's lengths add up to between half of 8192 and 8192, the rest of the row being padding. In each aligned group of 4 rows, one row holds a single sequence of 8192 positions and one row exactly two sequences; every other row holds two to four sequences.
All inputs are finite; a program needn't handle non-finite values.
Results may differ from a plain program's by a relative error of at most 0.0059.
Values may be sent and summed in bfloat16 or wider, within the bound.
A program may use at most 320 MiB of HBM per device.

v0:
```python
import jax
import jax.numpy as jnp
from jax import lax
from jax.sharding import PartitionSpec as P

BLOCK = 256


EPS = 1e-05
HIGHEST = lax.Precision.HIGHEST


def from_behind(array, axis, by):
    length = lax.axis_size(axis)
    pairs = [(i, i + by) for i in range(length) if 0 <= i + by < length]
    return lax.ppermute(array, axis, pairs)


def entering_2(array, axis, combine, identity, reverse):
    length, mine = (lax.axis_size(axis), lax.axis_index(axis))
    everything = jax.tree.map(lambda part: lax.all_gather(part, axis), array)
    start = jax.tree.map(
        lambda part, zero: jnp.broadcast_to(jnp.asarray(zero, part.dtype), part.shape),
        array,
        identity,
    )

    def step(k, before):
        at = length - 1 - k if reverse else k
        reached = at > mine if reverse else at < mine
        new = combine(before, jax.tree.map(lambda part: part[at], everything))
        return jax.tree.map(lambda a, b: jnp.where(reached, a, b), new, before)

    return lax.fori_loop(0, length, step, start)


def segment_ids(lengths, position_index):
    ends = jnp.cumsum(lengths, axis=1)
    segment = jnp.sum((ends[:, None, :] <= position_index[None, :, None]).astype(jnp.int32), axis=2)
    valid = position_index[None, :] < ends[:, -1:]
    return (segment, valid)


def rms_scale(value_rows, gain):
    return (
        value_rows
        * lax.rsqrt(jnp.mean(value_rows * value_rows, axis=-1, keepdims=True) + EPS)
        * gain
    )


def gated_norm(mixer_layer, gate, gain):
    return rms_scale(mixer_layer * jax.nn.silu(gate), gain)


def causal_conv(padded, kernel, offset, segment):
    width = kernel.shape[0]
    length_value = padded.shape[1] - width + 1
    own = segment[:, width - 1 :]
    total = offset
    for index in range(width):
        same = (segment[:, index : index + length_value] == own)[..., None]
        total = (
            total + jnp.where(same, padded[:, index : index + length_value], 0.0) * kernel[index]
        )
    return jax.nn.silu(total)


def rates(step_raw, dt_bias, a_log):
    step = jax.nn.softplus(step_raw + dt_bias)
    return (step, -step * jnp.exp(a_log))


def block_parts(value_rows, in_map, out_map, step, log_decay, segment, segment_prev):
    batch, length_value, heads, head_dim = value_rows.shape
    count = length_value // BLOCK
    blocked = value_rows.reshape(batch, count, BLOCK, heads, head_dim)
    inputs = in_map.reshape(batch, count, BLOCK, -1)
    readout = out_map.reshape(batch, count, BLOCK, -1)
    steps = step.reshape(batch, count, BLOCK, heads)
    running = jnp.cumsum(log_decay.reshape(batch, count, BLOCK, heads), axis=2)
    labels = segment.reshape(batch, count, BLOCK)
    before = jnp.concatenate([segment_prev[:, None], labels[:, :-1, -1]], axis=1)
    order = jnp.arange(BLOCK)
    inside = (
        (labels[:, :, :, None] == labels[:, :, None, :]) & (order[:, None] >= order[None, :])
    )[:, :, None]
    turned = jnp.moveaxis(running, 3, 2)
    spread = turned[..., :, None] - turned[..., None, :]
    decay = jnp.where(inside, jnp.exp(jnp.where(inside, spread, 0.0)), 0.0)
    scores = jnp.einsum("rkqn,rksn->rkqs", readout, inputs, precision=HIGHEST)
    mixing = decay * scores[:, :, None] * jnp.moveaxis(steps, 3, 2)[:, :, :, None, :]
    inner = jnp.einsum("rkhqs,rkshp->rkqhp", mixing, blocked, precision=HIGHEST)
    last = labels[:, :, -1]
    keep = (labels == last[:, :, None])[..., None]
    tail = (
        jnp.where(keep, jnp.exp(jnp.where(keep, running[:, :, -1:, :] - running, 0.0)), 0.0) * steps
    )
    local_state = jnp.einsum(
        "rkshp,rksn->rkhpn", blocked * tail[..., None], inputs, precision=HIGHEST
    )
    carry = jnp.where((last == before)[..., None], jnp.exp(running[:, :, -1, :]), 0.0)
    entry = jnp.where((labels == before[:, :, None])[..., None], jnp.exp(running), 0.0)
    return (inner, local_state, carry, entry, readout)


def block_chain(local_state, carry, state_in):

    def advance(state, item):
        factor, fresh = item
        return (factor[:, :, None, None] * state + fresh, state)

    final, entering = lax.scan(
        advance, state_in, (jnp.moveaxis(carry, 1, 0), jnp.moveaxis(local_state, 1, 0))
    )
    return (final, jnp.moveaxis(entering, 0, 1))


def block_output(inner, entry, readout, entering):
    carried = entry[..., None] * jnp.einsum(
        "rkqn,rkhpn->rkqhp", readout, entering, precision=HIGHEST
    )
    batch, count, width, heads, head_dim = inner.shape
    return (inner + carried).reshape(batch, count * width, heads, head_dim)


def product_over_blocks(carry):
    through = carry[:, 0]
    for index in range(1, carry.shape[1]):
        through = through * carry[:, index]
    return through


def all_pieces(
    value_rows, in_map, out_map, step_raw, dt_bias, a_log, segment, segment_prev, state_in
):
    step, log_decay = rates(step_raw, dt_bias, a_log)
    inner, local_state, carry, entry, readout = block_parts(
        value_rows, in_map, out_map, step, log_decay, segment, segment_prev
    )
    own_final, unused = block_chain(local_state, carry, jnp.zeros_like(state_in))
    final, entering = block_chain(local_state, carry, state_in)
    output = block_output(inner, entry, readout, entering)
    return (output, product_over_blocks(carry), own_final)


def combine_states(earlier, later):
    return (earlier[0] * later[0], later[0][:, :, None, None] * earlier[1] + later[1])


def body(
    hidden,
    lengths,
    cotangent,
    norm_gain,
    in_proj,
    conv_weight,
    conv_bias,
    a_log,
    dt_bias,
    skip_weight,
    inner_gain,
    out_proj,
):
    gathered = (
        lax.all_gather(norm_gain, ("row", "seq"), axis=0, tiled=True),
        lax.all_gather(in_proj, ("row", "seq"), axis=0, tiled=True),
        lax.all_gather(conv_weight, ("row", "seq"), axis=1, tiled=True),
        lax.all_gather(conv_bias, ("row", "seq"), axis=0, tiled=True),
        lax.all_gather(inner_gain, ("row", "seq"), axis=0, tiled=True),
        lax.all_gather(out_proj, ("row", "seq"), axis=0, tiled=True),
    )
    norm_full, proj_full, kernel_full, offset_full, inner_full, out_full = gathered
    batch, length_value, model = hidden.shape
    width = kernel_full.shape[0]
    heads = a_log.shape[0]
    inner_width = out_full.shape[0]
    channels = kernel_full.shape[1]
    state = (channels - inner_width) // 2
    head_dim = inner_width // heads
    start = lax.axis_index("seq") * length_value
    position_index = start + jnp.arange(length_value, dtype=jnp.int32)
    segment, valid = segment_ids(lengths, position_index)
    wider, unused = segment_ids(
        lengths, start - (width - 1) + jnp.arange(length_value + width - 1, dtype=jnp.int32)
    )
    segment_prev = wider[:, width - 2]
    residual = hidden.astype(jnp.float32)
    normed = rms_scale(residual, norm_full.astype(jnp.float32)).astype(jnp.bfloat16)
    gate = jnp.einsum(
        "rtd,de->rte", normed, proj_full[:, :inner_width], preferred_element_type=jnp.float32
    )
    mixed_in = jnp.einsum(
        "rtd,de->rte",
        normed,
        proj_full[:, inner_width : inner_width + channels],
        preferred_element_type=jnp.float32,
    )
    step_raw = jnp.einsum(
        "rtd,de->rte",
        normed,
        proj_full[:, inner_width + channels :],
        preferred_element_type=jnp.float32,
    )
    edge = from_behind(mixed_in[:, length_value - (width - 1) :], "seq", 1)
    padded = jnp.concatenate([edge, mixed_in], axis=1)
    active_flag = causal_conv(
        padded, kernel_full.astype(jnp.float32), offset_full.astype(jnp.float32), wider
    )
    value_rows = active_flag[..., :inner_width].reshape(batch, length_value, heads, head_dim)
    in_map = active_flag[..., inner_width : inner_width + state]
    out_map = active_flag[..., inner_width + state :]

    def row_pieces(item):
        values_row, in_row, out_row, raw_row, label_row, prev_row = item
        step, log_decay = rates(raw_row[None], dt_bias, a_log)
        inner, local_state, carry, entry, readout = block_parts(
            values_row[None],
            in_row[None],
            out_row[None],
            step,
            log_decay,
            label_row[None],
            prev_row[None],
        )
        own_final, unused_row = block_chain(local_state, carry, jnp.zeros_like(local_state[:, 0]))
        return (
            product_over_blocks(carry)[0],
            own_final[0],
            inner[0],
            local_state[0],
            carry[0],
            entry[0],
        )

    through, local_final, kept_inner, kept_local, kept_carry, kept_entry = lax.map(
        row_pieces, (value_rows, in_map, out_map, step_raw, segment, segment_prev)
    )
    kept_readout = out_map.reshape(batch, kept_inner.shape[1], kept_inner.shape[2], -1)
    identity = (jnp.ones_like(through), jnp.zeros_like(local_final))
    inbound = entering_2((through, local_final), "seq", combine_states, identity, False)[1]

    def carried_output(state_arg):
        unused_final, entering = block_chain(kept_local, kept_carry, state_arg)
        return block_output(kept_inner, kept_entry, kept_readout, entering)

    scanned_state, pull_state = jax.vjp(carried_output, inbound)
    mixer_layer = (scanned_state + skip_weight[:, None] * value_rows).reshape(
        batch, length_value, inner_width
    )
    gated = gated_norm(mixer_layer, gate, inner_full.astype(jnp.float32)).astype(jnp.bfloat16)
    branch = jnp.einsum("rti,id->rtd", gated, out_full, preferred_element_type=jnp.float32)
    block_out = jnp.where(valid[..., None], residual + branch, 0.0).astype(jnp.bfloat16)
    weights_back = (
        lax.all_gather(norm_gain, ("row", "seq"), axis=0, tiled=True),
        lax.all_gather(in_proj, ("row", "seq"), axis=0, tiled=True),
        lax.all_gather(conv_weight, ("row", "seq"), axis=1, tiled=True),
        lax.all_gather(conv_bias, ("row", "seq"), axis=0, tiled=True),
        lax.all_gather(inner_gain, ("row", "seq"), axis=0, tiled=True),
        lax.all_gather(out_proj, ("row", "seq"), axis=0, tiled=True),
    )
    norm_back, proj_back, kernel_back, offset_back, inner_back, out_back = weights_back
    masked = jnp.where(valid[..., None], cotangent.astype(jnp.float32), 0.0)
    masked_low = masked.astype(jnp.bfloat16)
    out_proj_grad = jnp.einsum("rti,rtd->id", gated, masked_low, preferred_element_type=jnp.float32)
    gated_back = jnp.einsum("rtd,id->rti", masked_low, out_back, preferred_element_type=jnp.float32)
    unused_out, pull_gated = jax.vjp(gated_norm, mixer_layer, gate, inner_back.astype(jnp.float32))
    mixer_back, gate_back, inner_gain_grad = pull_gated(gated_back)
    heads_back = mixer_back.reshape(batch, length_value, heads, head_dim)
    skip_grad = jnp.sum(heads_back * value_rows, axis=(0, 1, 3))
    leaving = pull_state(heads_back)[0]
    onward = entering_2((through, leaving), "seq", combine_states, identity, True)[1]
    through_back = jnp.sum(onward * inbound, axis=(2, 3))

    def row_pull(item):
        (
            values_row,
            in_row,
            out_row,
            raw_row,
            label_row,
            prev_row,
            state_row,
            grad_row,
            through_row,
            final_row,
        ) = item

        def local(values_arg, in_arg, out_arg, raw_arg, bias_arg, decay_arg):
            output, through_one, final_one = all_pieces(
                values_arg[None],
                in_arg[None],
                out_arg[None],
                raw_arg[None],
                bias_arg,
                decay_arg,
                label_row[None],
                prev_row[None],
                state_row[None],
            )
            return (output[0], through_one[0], final_one[0])

        unused_row, pull_row = jax.vjp(local, values_row, in_row, out_row, raw_row, dt_bias, a_log)
        return pull_row((grad_row, through_row, final_row))

    values_a, in_a, out_a, raw_a, bias_a, decay_a = lax.map(
        row_pull,
        (
            value_rows,
            in_map,
            out_map,
            step_raw,
            segment,
            segment_prev,
            inbound,
            heads_back,
            through_back,
            onward,
        ),
    )
    values_grad = values_a + skip_weight[:, None] * heads_back
    active_back = jnp.concatenate(
        [values_grad.reshape(batch, length_value, inner_width), in_a, out_a], axis=-1
    )

    def convolve(padded_arg, kernel_arg, offset_arg):
        return causal_conv(padded_arg, kernel_arg, offset_arg, wider)

    unused_conv, pull_conv = jax.vjp(
        convolve, padded, kernel_back.astype(jnp.float32), offset_back.astype(jnp.float32)
    )
    padded_back, conv_weight_grad, conv_bias_grad = pull_conv(active_back)
    returned = from_behind(padded_back[:, : width - 1], "seq", -1)
    mixed_back = padded_back[:, width - 1 :]
    mixed_back = jnp.concatenate(
        [
            mixed_back[:, : length_value - (width - 1)],
            mixed_back[:, length_value - (width - 1) :] + returned,
        ],
        axis=1,
    )
    gate_low = gate_back.astype(jnp.bfloat16)
    mixed_low = mixed_back.astype(jnp.bfloat16)
    raw_low = raw_a.astype(jnp.bfloat16)
    in_proj_grad = jnp.concatenate(
        [
            jnp.einsum("rtd,rte->de", normed, gate_low, preferred_element_type=jnp.float32),
            jnp.einsum("rtd,rte->de", normed, mixed_low, preferred_element_type=jnp.float32),
            jnp.einsum("rtd,rte->de", normed, raw_low, preferred_element_type=jnp.float32),
        ],
        axis=1,
    )
    normed_back = (
        jnp.einsum(
            "rte,de->rtd", gate_low, proj_back[:, :inner_width], preferred_element_type=jnp.float32
        )
        + jnp.einsum(
            "rte,de->rtd",
            mixed_low,
            proj_back[:, inner_width : inner_width + channels],
            preferred_element_type=jnp.float32,
        )
        + jnp.einsum(
            "rte,de->rtd",
            raw_low,
            proj_back[:, inner_width + channels :],
            preferred_element_type=jnp.float32,
        )
    )
    unused_norm, pull_norm = jax.vjp(rms_scale, residual, norm_back.astype(jnp.float32))
    residual_back, norm_gain_grad = pull_norm(normed_back)
    hidden_grad = (masked + residual_back).astype(jnp.bfloat16)
    grads = (
        lax.psum_scatter(norm_gain_grad, ("row", "seq"), scatter_dimension=0, tiled=True),
        lax.psum_scatter(in_proj_grad, ("row", "seq"), scatter_dimension=0, tiled=True),
        lax.psum_scatter(conv_weight_grad, ("row", "seq"), scatter_dimension=1, tiled=True),
        lax.psum_scatter(conv_bias_grad, ("row", "seq"), scatter_dimension=0, tiled=True),
        lax.psum_scatter(inner_gain_grad, ("row", "seq"), scatter_dimension=0, tiled=True),
        lax.psum_scatter(out_proj_grad, ("row", "seq"), scatter_dimension=0, tiled=True),
    )
    head_sums = lax.psum(
        (jnp.sum(decay_a, axis=0), jnp.sum(bias_a, axis=0), skip_grad), ("row", "seq")
    )
    return (
        block_out,
        hidden_grad,
        grads[0],
        grads[1],
        grads[2],
        grads[3],
        head_sums[0],
        head_sums[1],
        head_sums[2],
        grads[4],
        grads[5],
    )


def solution(mesh):
    return jax.shard_map(
        body,
        mesh=mesh,
        in_specs=(
            P("row", "seq", None),
            P("row", None),
            P("row", "seq", None),
            P(("row", "seq")),
            P(("row", "seq"), None),
            P(None, ("row", "seq")),
            P(("row", "seq")),
            P(),
            P(),
            P(),
            P(("row", "seq")),
            P(("row", "seq"), None),
        ),
        out_specs=(
            P("row", "seq", None),
            P("row", "seq", None),
            P(("row", "seq")),
            P(("row", "seq"), None),
            P(None, ("row", "seq")),
            P(("row", "seq")),
            P(),
            P(),
            P(),
            P(("row", "seq")),
            P(("row", "seq"), None),
        ),
        check_vma=False,
    )
```

profile of v0, /device:TPU:0, one launch (start us, length us, event | category | flops | bytes accessed | tf_op | source)
XLA Modules:
  0.0 867.5 jit_solution(7488918105238420933)
XLA Ops:
  12.1 42.4 %all-reduce.23 = (bf16[768]{0:T(1024)(128)(2,1)S(1)}, bf16[1792]{0:T(1024)(128)(2,1)S(1)}, bf16[1536]{0:T(1024)(128)(2,1)}) all-reduce(bf16[768]{0:T(1024)(128)(2,1)S(1)} %dynamic-update-slice.1, bf16[1792]{0:T(1024)(128)(2,1)S(1)} %dynamic-update-slice, ...), channel_id=1, replica_groups=mesh['row'=4,'seq'=8] {'row','seq'}, use_global_device_ids=true, to_apply=%add.15 | all-reduce | flops 4096 | bytes 16384
  55.2 66.7 %all-gather.2 = bf16[32,56,4]{1,2,0:T(4,128)(2,1)S(1)} all-gather(bf16[1,56,4]{1,2,0:T(4,128)(2,1)} %bitcast.406), channel_id=1, replica_groups=mesh['row'=4,'seq'=8] {'row','seq'}, dimensions={0}, use_global_device_ids=true | all-gather | bytes 14784 | tf_op jit(solution)/shard_map/all_gather | solution.py:168
  201.4 19.0 %all_gather.46 = f32[8,1,24]{2,1,0:T(1,128)S(1)} all-gather(f32[1,1,24]{2,1,0:T(1,128)S(1)} %slice_multiply_fusion), channel_id=1, replica_groups=mesh['row'=4,'seq'=8] {'seq'}, dimensions={0}, use_global_device_ids=true | all-gather | bytes 864 | tf_op jit(solution)/shard_map/all_gather | solution.py:21
  221.0 10.0 %reshape.1204 = f32[1,4,256,24,64]{4,3,2,1,0:T(8,128)} reshape(f32[1,1024,1536]{2,1,0:T(8,128)} %slice.193) | data formatting | bytes 12582912 | tf_op jit(solution)/shard_map/while/body/eval_jaxpr/reshape;while/body/eval_jaxpr/broadcast_in_dim | solution.py:77
  231.0 10.0 %copy.307 = f32[1,4,256,24,64]{2,4,3,1,0:T(8,128)} copy(f32[1,4,256,24,64]{4,3,2,1,0:T(8,128)} %reshape.1204) | data formatting | bytes 12582912 | tf_op jit(solution)/shard_map/while/body/eval_jaxpr/reshape;while/body/eval_jaxpr/broadcast_in_dim | solution.py:77
  244.0 46.7 %all-gather.12.cloned.1.call-done = f32[8,24,64,128]{3,2,1,0:T(8,128)} async-done(((f32[1,24,64,128]{3,2,1,0:T(8,128)}), f32[8,24,64,128]{3,2,1,0:T(8,128)}) %all-gather.12.cloned.1.call-update) | async-done | bytes 6291472 | tf_op jit(solution)/shard_map/all_gather | solution.py:21
  290.7 10.7 %while.168 = (s32[]{:T(128)}, f32[1,24,64,128]{3,2,1,0:T(8,128)S(1)}, s32[]{:T(128)}, f32[8,1,24]{2,1,0:T(1,128)S(1)}, f32[8,1,24,64,128]{4,3,2,1,0:T(8,128)}, /*index=5*/s32[]{:T(128)}, s32[]{:T(128)}) while((s32[]{:T(128)}, f32[1,24,64,128]{3,2,1,0:T(8,128)S(1)}, s32[]{:T(128)}, f32[8,1,24]{2,1,0:T(1,128)S(1)}, ...), condition=%wide.region_9.10_spmd.clone, body=%wide.region_8.9_spmd.clone.sunk | while | flops 786436 | bytes 2359697 | solution.py:34
  322.8 32.7 %bitcast_add_fusion.9 = f32[4,256,24,64]{1,3,2,0:T(8,128)} fusion(f32[4,256,24,64]{1,3,2,0:T(8,128)S(1)} %fusion.70, f32[4,256,24]{1,2,0:T(8,128)S(1)} %bitcast.381, f32[4,24,256]{2,1,0:T(8,128)S(1)} %copy-done.55, f32[4,256,256]{2,1,0:T(8,128)S(1)} %copy-done.38, f32[4,24,256]{2,1,0:T(8,128)S(1)} %copy-done.59, pred[4,256,256]{2,1,0:T(8,128)(4,1)S(1)} %copy-done.48, ...), kind=kOutput, calls=%fused_computation.90 | convolution fusion | flops 4866441216 | bytes 20480000 | tf_op jit(solution)/shard_map/while/body/eval_jaxpr/rkhqs,rkshp->rkqhp/dot_general | solution.py:93
  365.3 11.2 %reshape.1202 = f32[1024,1536]{1,0:T(8,128)} reshape(f32[4,256,24,64]{3,2,1,0:T(8,128)} %copy.326) | data formatting | bytes 12582912 | tf_op jit(solution)/shard_map/jvp()/reshape | solution.py:124
  376.5 11.4 %multiply_reduce_fusion.9 = (f32[1024]{0:T(1024)S(1)}, f32[1024,1536]{1,0:T(8,128)}, f32[1024,1536]{1,0:T(8,128)}) fusion(f32[1024,1536]{1,0:T(8,128)} %reshape.1202, f32[1,1024,1792]{2,1,0:T(8,128)} %copy-done.2, f32[1536]{0:T(1024)S(1)} %copy-done.78, bf16[768,3352]{1,0:T(8,128)(2,1)} %all-gather.8.cloned.1.call-done, bf16[1,1024,768]{2,1,0:T(8,128)(2,1)} %param.28, ...), kind=kOutput, calls=%fused_computation.103 | convolution fusion | flops 2433219584 | bytes 29115392 | tf_op jit(solution)/shard_map/rtd,de->rte/dot_general | solution.py:190
  420.6 10.6 %fusion.94 = f32[4,1,24,64,128]{4,3,2,1,0:T(8,128)} fusion(f32[4,256,128,1]{2,1,3,0:T(8,128)S(1)} %bitcast.366, f32[4,256,24,64]{1,0,3,2:T(4,128)} %broadcast_in_dim.500, f32[4,256,24]{1,2,0:T(8,128)S(1)} %bitcast.382), kind=kOutput, calls=%fused_computation.160 | convolution fusion | flops 2417491968 | bytes 10059776 | tf_op jit(solution)/shard_map/while/body/eval_jaxpr/transpose(jvp(rkqn,rkhpn->rkqhp))/dot_general | solution.py:120
  456.9 14.0 %fusion.104 = f32[4,256,128]{2,1,0:T(8,128)} fusion(f32[4,1,24,64,128]{4,3,2,1,0:T(8,128)S(1)} %copy-done.5, f32[4,256,24,64]{1,0,3,2:T(4,128)} %broadcast_in_dim.500, f32[4,256,24]{1,2,0:T(8,128)S(1)} %bitcast.383), kind=kOutput, calls=%fused_computation.167 | convolution fusion | flops 2417491968 | bytes 10059776 | tf_op jit(solution)/shard_map/while/body/eval_jaxpr/transpose(jvp(rkqn,rkhpn->rkqhp))/dot_general | solution.py:120
  483.0 44.1 %fusion.16 = (f32[4,24,256]{2,1,0:T(8,128)}, f32[4,24,256]{2,1,0:T(8,128)}, f32[4,24,256]{2,1,0:T(8,128)}, f32[4,256,256]{2,1,0:T(8,128)S(1)}) fusion(f32[4,24,256]{2,1,0:T(8,128)S(1)} %copy-done.56, f32[4,256,256]{2,1,0:T(8,128)S(1)} %copy-done.39, f32[4,24,256]{2,1,0:T(8,128)S(1)} %copy-done.60, pred[4,256,256]{2,1,0:T(8,128)(4,1)S(1)} %copy-done.48, ...), kind=kOutput, calls=%fused_computation.46 | convolution fusion | flops 4925874176 | bytes 15433728 | tf_op jit(solution)/shard_map/while/body/eval_jaxpr/transpose(jvp(rkhqs,rkshp->rkqhp))/dot_general | solution.py:93
  529.2 10.7 %while.169 = (s32[]{:T(128)}, f32[1,24,64,128]{3,2,1,0:T(8,128)S(1)}, f32[4,1,24]{2,1,0:T(1,128)S(1)}, f32[4,1,24,64,128]{4,3,2,1,0:T(8,128)}, f32[4,1,24,64,128...) while((s32[]{:T(128)}, ...), condition=%wide.region_16.17_spmd.clone, body=%wide.region_14.16_spmd.clone.sunk | while | flops 1179628 | bytes 4720148 | solution.py:113
  541.9 11.0 %while.171 = (s32[]{:T(128)}, f32[1,24,64,128]{3,2,1,0:T(8,128)S(1)}, s32[]{:T(128)}, f32[8,1,24]{2,1,0:T(1,128)S(1)}, f32[8,1,24,64,128]{4,3,2,1,0:T(8,128)}, /*index=5*/s32[]{:T(128)}, s32[]{:T(128)}, s32[]{:T(128)}, s32[]{:T(128)}) while((s32[]{:T(128)}, f32[1,24,64,128]{3,2,1,0:T(8,128)S(1)}, s32[]{:T(128)}, ...), condition=%wide.region_20.21_spmd.clone, body=%wide.region_19.20_spmd.clone.sunk | while | flops 786440 | bytes 2359759 | solution.py:34
  555.3 10.1 %while.166 = (s32[]{:T(128)}, f32[1,24,64,128]{3,2,1,0:T(8,128)S(1)}, f32[4,1,24]{2,1,0:T(1,128)S(1)}, f32[4,1,24,64,128]{4,3,2,1,0:T(8,128)}, f32[4,1,24,1,1]{2...) while((s32[]{:T(128)}, f32[1,24,64,128]{3,2,1,0:T(8,128)S(1)}, ...), condition=%wide.region_25.26_spmd, body=%wide.region_23.25_spmd.sunk | while | flops 589803 | bytes 3933681 | solution.py:113
  565.5 11.1 %fusion.107 = f32[1,4,256,128]{2,3,1,0:T(8,128)S(1)} fusion(f32[4,256,24,64]{1,0,3,2:T(4,128)} %copy-done.6, f32[4,1,24,64,128]{4,3,2,1,0:T(8,128)} %get-tuple-element.792, f32[4,1,24,64,128]{4,3,2,1,0:T(8,128)} %get-tuple-element.797), kind=kOutput, calls=%fused_computation.169 | convolution fusion | flops 2416705536 | bytes 13107200 | tf_op jit(solution)/shard_map/while/body/eval_jaxpr/transpose(jvp(rkshp,rksn->rkhpn))/dot_general | solution.py:99
  583.6 23.7 %bitcast_add_fusion.8 = f32[1,4,256,24,64]{2,4,3,1,0:T(8,128)} fusion(f32[4,24,64,256]{3,2,1,0:T(8,128)S(1)} %fusion.67, f32[4,256,24]{1,2,0:T(8,128)S(1)} %bitcast.387, f32[4,24,256]{2,1,0:T(8,128)S(1)} %copy-done.57, f32[4,256,256]{2,1,0:T(8,128)S(1)} %copy-done.40, f32[4,24,256]{2,1,0:T(8,128)S(1)} %copy-done.61, ...), kind=kOutput, calls=%fused_computation.89 | convolution fusion | flops 4866441216 | bytes 20480000 | tf_op jit(solution)/shard_map/while/body/eval_jaxpr/transpose(jvp(rkhqs,rkshp->rkqhp))/dot_general | solution.py:93
  611.7 10.0 %reduce-window.16 = f32[1,4,24,2,128]{4,2,3,1,0:T(8,128)S(1)} reduce-window(f32[1,4,24,2,128]{4,2,3,1,0:T(8,128)S(1)} %copy.313, f32[]{:T(128)} %constant.360.clone.1), window={size=1x1x1x1x128 pad=0_0x0_0x0_0x0_0x0_127}, to_apply=%region_34.35 | reduce-window | flops 3121152 | bytes 196612 | tf_op jit(solution)/shard_map/reduce-window.2
  631.8 11.4 %reshape.1203 = f32[1024,1536]{1,0:T(8,128)} reshape(f32[1,4,256,24,64]{4,3,2,1,0:T(8,128)} %copy.327) | data formatting | bytes 12582912 | tf_op jit(solution)/shard_map/while/body/eval_jaxpr/transpose(jvp())/reshape | solution.py:77
  643.3 18.0 %fusion.39 = (bf16[1024,1536]{1,0:T(8,128)(2,1)}, f32[1,1024,1536]{2,1,0:T(8,128)S(1)}) fusion(f32[1024,1536]{1,0:T(8,128)} %get-tuple-element.1295, f32[1024,1536]{1,0:T(8,128)} %get-tuple-element.1265, f32[1024]{0:T(1024)S(1)} %multiply_multiply_fusion.1, f32[1024,1536]{1,0:T(8,128)} %copy-done.15, f32[1536]{0:T(1024)S(1)} %convert_element_type.83, ...), kind=kLoop, calls=%fused_computation.88 | loop fusion | flops 31457280 | bytes 53497856 | tf_op jit(solution)/shard_map/convert_element_type | solution.py:342
  661.4 12.8 %multiply_reduce_fusion.4 = (f32[1792]{0:T(1024)}, f32[1792]{0:T(1024)}, f32[1792]{0:T(1024)}, f32[1792]{0:T(1024)}, f32[1792]{0:T(1024)}, /*index=5*/f32[1,1024,1792]{2,1,0:T(8,128)}) fusion(f32[1,1024,1792]{2,1,0:T(8,128)S(1)} %bitcast.359, f32[1,3,1792]{2,1,0:T(4,128)S(1)} %copy-done.53, pred[1024]{0:T(1024)(128)(4,1)S(1)} %copy-done.93, ...), kind=kLoop, calls=%fused_computation.79 | loop fusion | flops 47701248 | bytes 36760576 | tf_op jit(solution)/shard_map/transpose(jvp())/reduce_sum | solution.py:64
  740.5 41.6 %all-reduce.22 = (f32[768]{0:T(1024)S(1)}, f32[4,1792]{1,0:T(4,128)S(1)}, f32[1792]{0:T(1024)S(1)}, f32[24]{0:T(128)}, f32[24]{0:T(128)}, /*index=5*/f32[24]{0:T(128)}, f32[1536]{0:T(1024)S(1)}) all-reduce(f32[768]{0:T(1024)S(1)} %get-tuple-element.1150, ...), channel_id=4, replica_groups=mesh['row'=4,'seq'=8] {'row','seq'}, use_global_device_ids=true, to_apply=%region_38.39.clone | all-reduce | flops 11336 | bytes 90688
  788.1 72.3 %reduce-scatter.8.cloned.1.call-done = f32[24,3352]{1,0:T(8,128)} async-done(((f32[768,3352]{1,0:T(8,128)}), f32[24,3352]{1,0:T(8,128)}) %reduce-scatter.8.cloned.1.call-update) | async-done | bytes 321808
  (541 shorter events, 361.5 us)
Async XLA Ops:
  7.2 125.7 %copy-start.16 = (bf16[1,1024,768]{2,1,0:T(8,128)(2,1)S(1)}, bf16[1,1024,768]{2,1,0:T(8,128)(2,1)}, u32[]{:S(2)}) copy-start(bf16[1,1024,768]{2,1,0:T(8,128)(2,1)} %param.28) | copy-start | bytes 4718596
  7.2 118.9 %all-gather.8.cloned.1.call-start = ((), (), s32[]{:S(2)}) async-start(), calls=%async_computation.2 | async-start | bytes 5474304 | tf_op jit(solution)/shard_map/all_gather | solution.py:167
  7.9 282.8 %all-gather.12.cloned.1.call-start = ((), (), s32[]{:S(2)}) async-start(), calls=%async_computation.5 | async-start | bytes 7077888 | tf_op jit(solution)/shard_map/all_gather | solution.py:21
  8.9 120.2 %copy-start.72 = (s32[4,256]{1,0:T(4,128)}, s32[4,256]{1,0:T(4,128)S(1)}, u32[]{:S(2)}) copy-start(s32[4,256]{1,0:T(4,128)S(1)} %eq.136) | copy-start | bytes 12292
  9.6 119.5 %copy-start.112 = (f32[24]{0:T(128)}, f32[24]{0:T(128)S(1)}, u32[]{:S(2)}) copy-start(f32[24]{0:T(128)S(1)} %exp.90) | copy-start | bytes 292
  54.5 322.0 %copy-start.44 = (f32[768]{0:T(1024)}, f32[768]{0:T(1024)S(1)}, u32[]{:S(2)}) copy-start(f32[768]{0:T(1024)S(1)} %convert_element_type.79) | copy-start | bytes 9220
  126.1 250.4 %copy-start.46 = (f32[1024]{0:T(1024)}, f32[1024]{0:T(1024)S(1)}, u32[]{:S(2)}) copy-start(f32[1024]{0:T(1024)S(1)} %fusion.137) | copy-start | bytes 12292
  131.7 68.9 %copy-start.34 = (f32[1,4,256,24]{2,1,3,0:T(4,128)}, f32[1,4,256,24]{2,1,3,0:T(4,128)S(1)}, u32[]{:S(2)}) copy-start(f32[1,4,256,24]{2,1,3,0:T(4,128)S(1)} %reshape.1168) | copy-start | bytes 294916
  137.8 2.8 collective-permute-start
  191.7 196.2 %all-gather.10.cloned.1.call-start = ((), (), s32[]{:S(2)}) async-start(), calls=%async_computation.3 | async-start | bytes 2433024 | tf_op jit(solution)/shard_map/all_gather | solution.py:171
  192.5 349.4 %all-gather.14.cloned.1.call-start = ((), (), s32[]{:S(2)}) async-start(), calls=%async_computation.6 | async-start | bytes 7077888 | tf_op jit(solution)/shard_map/all_gather | solution.py:21
  200.6 20.4 %copy-start.86 = (f32[1,4,24]{2,1,0:T(4,128)}, f32[1,4,24]{2,1,0:T(4,128)S(1)}, u32[]{:S(2)}) copy-start(f32[1,4,24]{2,1,0:T(4,128)S(1)} %bitcast_select_fusion.1) | copy-start | bytes 1156
  437.3 350.8 %reduce-scatter.6.cloned.1.call-start = ((), (), s32[]{:S(2)}) async-start(), calls=%async_computation.4 | async-start | bytes 4866048 | tf_op jit(solution)/shard_map/reduce_scatter | solution.py:379
  456.9 20.7 %slice-start.4 = ((s8[6291456]{0:T(1024)(128)(4,1)}), s8[4194304]{0:T(1024)(128)(4,1)S(1)}, s32[]{:S(2)}) async-start(s8[6291456]{0:T(1024)(128)(4,1)} %bitcast.362), calls=%async_computation.12 | async-start | bytes 8388608
  483.0 46.1 %copy-start.3 = (f32[1,24,64,128]{3,2,1,0:T(8,128)S(1)}, f32[1,24,64,128]{3,2,1,0:T(8,128)}, u32[]{:S(2)}) copy-start(f32[1,24,64,128]{3,2,1,0:T(8,128)} %custom-call.2) | copy-start | bytes 2359300
  483.0 46.1 %copy-start.89 = (f32[4,1,24]{2,0,1:T(4,128)S(1)}, f32[4,1,24]{2,0,1:T(4,128)}, u32[]{:S(2)}) copy-start(f32[4,1,24]{2,0,1:T(4,128)} %copy-done.88) | copy-start | bytes 1156
  539.9 320.6 %reduce-scatter.8.cloned.1.call-start = ((), (), s32[]{:S(2)}) async-start(), calls=%async_computation.7 | async-start | bytes 10948608
  576.7 30.6 %slice-start.2 = ((s8[6291456]{0:T(1024)(128)(4,1)}), s8[4194304]{0:T(1024)(128)(4,1)S(1)}, s32[]{:S(2)}) async-start(s8[6291456]{0:T(1024)(128)(4,1)} %bitcast.360), calls=%async_computation.10 | async-start | bytes 8388608
  583.6 23.8 %slice-start.3 = ((s8[6291456]{0:T(1024)(128)(4,1)}), s8[2097152]{0:T(1024)(128)(4,1)S(1)}, s32[]{:S(2)}) async-start(s8[6291456]{0:T(1024)(128)(4,1)} %bitcast.360), calls=%async_computation.11 | async-start | bytes 4194304
  631.8 29.5 %slice-start = ((s8[7340032]{0:T(1024)(128)(4,1)}), s8[3145728]{0:T(1024)(128)(4,1)S(1)}, s32[]{:S(2)}) async-start(s8[7340032]{0:T(1024)(128)(4,1)} %bitcast.357), calls=%async_computation.8 | async-start | bytes 6291456
  643.2 18.1 %copy-start.91 = (pred[1024]{0:T(1024)(128)(4,1)S(1)}, pred[1024]{0:T(1024)(128)(4,1)}, u32[]{:S(2)}) copy-start(pred[1024]{0:T(1024)(128)(4,1)} %copy-done.90) | copy-start | bytes 3076
  684.8 18.6 %collective-permute-start.1 = (f32[1,3,1792]{2,1,0:T(4,128)}, f32[1,3,1792]{2,1,0:T(4,128)}, u32[]{:S(2)}, u32[]{:S(2)}) collective-permute-start(f32[1,3,1792]{2,1,0:T(4,128)} %pad_add_fusion.1), channel_id=1, source_target_pairs={{1,0},{2,1},{3,2},{4,3},{5,4},{6,5},{7,6},{9,8},{10,9},{11,10},{12... | collective-permute-start | bytes 64520 | tf_op jit(solution)/shard_map/ppermute | solution.py:16
  733.6 50.9 %copy-start.74 = (f32[1024]{0:T(1024)S(1)}, f32[1024]{0:T(1024)}, u32[]{:S(2)}) copy-start(f32[1024]{0:T(1024)} %copy-done.73) | copy-start | bytes 12292
  733.7 50.9 %copy-start.37 = (bf16[1,1024,768]{2,1,0:T(8,128)(2,1)S(1)}, bf16[1,1024,768]{2,1,0:T(8,128)(2,1)}, u32[]{:S(2)}) copy-start(bf16[1,1024,768]{2,1,0:T(8,128)(2,1)} %param.30) | copy-start | bytes 4718596
  (108 other events, 890.0 us)
Sparse Core Ops, SparseCore 0:
  10.9 68.4 all-gather.7
  191.9 98.8 all-gather.11
  293.6 55.5 all-gather.9
  437.5 97.1 all-gather.13
  540.6 105.1 reduce-scatter.5
  717.9 142.4 reduce-scatter.7
where the time goes:
time: 877 us; the launch traced here: 868 us
  matrix products  225 us (26%)
  other arithmetic  183 us (21%)
  blocking collectives  170 us (19%)
  local copies, waits for them, and re-layouts  148 us (17%)
  waiting for transfers between devices  121 us (14%)
  between operations  16.2 us (2%)
    dot_general x3, matrix products, block_parts(): inner = jnp.einsum('rkhqs,rkshp->rkqhp', mixing, blocked, precision=HIGHEST)  101 us
    unnamed x2, blocking collectives  83.9 us
    unnamed x7, waiting for transfers between devices  73.8 us
    all_gather x1, blocking collectives, body(): lax.all_gather(conv_weight, ('row', 'seq'), axis=1, tiled=True)  66.7 us
    all_gather x2, waiting for transfers between devices, entering_2(): everything = jax.tree.map(lambda part: lax.all_gather(part, axis), array)  46.7 us
    dot_general x3, matrix products, block_output(): jnp.einsum('rkqn,rkhpn->rkqhp', readout, entering, precision=HIGHEST)  31.9 us
    dot_general x3, matrix products, block_parts(): jnp.einsum('rkshp,rksn->rkhpn', blocked * tail[..., None], inputs, precis...  22.3 us
    reshape x2, local copies, waits for them, and re-layouts, block_parts(): blocked = value_rows.reshape(batch, count, BLOCK, heads, head_dim)  21.3 us
  transfers between devices with their start and end apart: 8, of which 3 were waited for; matrix products, arithmetic and copies ran while one was open for 51% of the time, Pallas kernels for 0%

commit v1 on v0

v1 whole, which is shorter than its diff:
```python
import functools

import jax
import jax.numpy as jnp
from jax import lax
from jax.experimental import pallas as pl
from jax.experimental.pallas import tpu as pltpu
from jax.sharding import PartitionSpec as P

BLOCK = 256
EPS = 1e-05
LOG2E = 1.4426950408889634
HIGHEST = lax.Precision.HIGHEST
F32 = jnp.float32
LOW = jnp.bfloat16
EDGE = 8
HALO = 16
AXES = ("row", "seq")
MESH = pl.DeviceIdType.MESH
CORES = 2
DEPTH = 4
VMEM_BYTES = 63 * 1024 * 1024


def nn(a, b, precision=None):
    return lax.dot_general(
        a, b, (((1,), (0,)), ((), ())), precision=precision, preferred_element_type=F32
    )


def nt(a, b):
    return lax.dot_general(a, b, (((1,), (1,)), ((), ())), preferred_element_type=F32)


def tn(a, b, precision=None):
    return lax.dot_general(
        a, b, (((0,), (0,)), ((), ())), precision=precision, preferred_element_type=F32
    )


def halves(v):
    high = v.astype(LOW)
    return high, (v - high.astype(F32)).astype(LOW)


def head_groups(heads, width):
    column = lax.broadcasted_iota(jnp.int32, (heads, width), 1)
    first = lax.broadcasted_iota(jnp.int32, (heads, width), 0) * (width // heads)
    return ((column >= first) & (column < first + width // heads)).astype(F32).astype(LOW)


def spread(v, groups):
    high, rest = halves(v)
    return nn(high, groups) + nn(rest, groups)


def head_sums(v, groups):
    high, rest = halves(v)
    return nt(high, groups) + nt(rest, groups)


def triangle():
    return (
        lax.broadcasted_iota(jnp.int32, (BLOCK, BLOCK), 0) >= lax.broadcasted_iota(jnp.int32, (BLOCK, BLOCK), 1)
    ).astype(F32)


def sigmoid(v):
    return 0.5 + 0.5 * jnp.tanh(0.5 * v)


def log1p_of(v):
    series = v * (1.0 - v * (0.5 - v * (1.0 / 3.0 - 0.25 * v)))
    return jnp.where(v < 0.01, series, jnp.log(1.0 + v))


def rms_rate(v):
    return lax.rsqrt(jnp.mean(v * v, axis=-1, keepdims=True) + EPS)


class Labels:
    def __init__(self, info, block, rows=BLOCK):
        slots = info.shape[1] - 1
        self.ends, total = [], 0
        for i in range(slots):
            total = total + info[0, i]
            self.ends.append(total)
        self.base = info[0, slots] + block * BLOCK
        self.rows = rows

    def of(self, place):
        total = sum((place >= end).astype(jnp.int32) for end in self.ends)
        return jnp.where(place < 0, -1, total)

    def column(self):
        return self.of(self.base + lax.broadcasted_iota(jnp.int32, (self.rows, 1), 0))

    def row(self):
        return self.of(self.base + lax.broadcasted_iota(jnp.int32, (1, self.rows), 1))

    def before(self):
        return self.of(self.base - 1)

    def last(self):
        return self.of(self.base + BLOCK - 1)

    def entry(self):
        return (self.column() == self.before()).astype(F32)

    def keep(self):
        return (self.column() == self.last()).astype(F32)

    def flag(self):
        return (jnp.full((8, 128), self.before(), jnp.int32) == self.last()).astype(F32)

    def valid(self):
        place = self.base + lax.broadcasted_iota(jnp.int32, (self.rows, 1), 0)
        return (place < self.ends[-1]).astype(F32)

    def same(self):
        shape = (self.rows, 8)
        place = self.base + lax.broadcasted_iota(jnp.int32, shape, 0)
        own = self.of(place)
        return (self.of(place - lax.broadcasted_iota(jnp.int32, shape, 1)) == own).astype(F32)


class Place:
    def __init__(self):
        rows, self.seqs = lax.axis_size("row"), lax.axis_size("seq")
        self.sx, self.sz = rows // CORES, DEPTH
        self.sy = self.seqs // DEPTH
        row, seq = lax.axis_index("row"), lax.axis_index("seq")
        self.x, self.core = lax.div(row, CORES), lax.rem(row, CORES)
        self.z, self.y = lax.div(seq, self.sy), lax.rem(seq, self.sy)
        self.row, self.seq = row, seq
        self.count = rows * self.seqs
        self.twin = self.device(core=1 - self.core)

    def device(self, x=None, core=None, z=None, y=None):
        x = self.x if x is None else x
        core = self.core if core is None else core
        z = self.z if z is None else z
        y = self.y if y is None else y
        return {"row": x * CORES + core, "seq": z * self.sy + y}

    def slot(self, x=None, core=None, z=None, y=None):
        at = self.device(x, core, z, y)
        return at["row"] * self.seqs + at["seq"]

    def peers(self, axis):
        size, mine = {"x": (self.sx, self.x), "y": (self.sy, self.y), "z": (self.sz, self.z)}[axis]
        return [(k, lax.rem(mine + k, size)) for k in range(1, size)]

    def around(self):
        return (
            [self.device(x=p) for _, p in self.peers("x")]
            + [self.device(y=p) for _, p in self.peers("y")]
            + [self.device(z=p) for _, p in self.peers("z")]
            + [self.twin]
        )

    def along(self, by):
        return {"seq": lax.rem(self.seq + by + self.seqs, self.seqs)}


def greet(devices):
    barrier = pltpu.get_barrier_semaphore()
    for device in devices:
        pl.semaphore_signal(barrier, inc=1, device_id=device, device_id_type=MESH)
    pl.semaphore_wait(barrier, len(devices))


def remote(source, target, send_sem, recv_sem, device):
    return pltpu.make_async_remote_copy(
        src_ref=source, dst_ref=target, send_sem=send_sem, recv_sem=recv_sem, device_id=device, device_id_type=MESH
    )


class Gather:
    def __init__(self, me, ins, outs, local_sem, send_sem, recv_sem):
        self.me, self.ins, self.outs = me, ins, outs
        self.local_sem, self.send_sem, self.recv_sem = local_sem, send_sem, recv_sem
        self.steps = [[self.plan(a, stage) for stage in range(4)] for a in range(len(ins))]

    def plan(self, a, stage):
        me = self.me
        xs = [p for _, p in me.peers("x")]
        ys = [p for _, p in me.peers("y")]
        zs = [p for _, p in me.peers("z")]
        around = [(me.device(y=p), None) for p in ys] + [(me.device(x=p), None) for p in xs] + [(me.twin, None)]
        if stage == 0:
            return [(None, [(me.device(z=p), None) for p in zs] + around)]
        if stage == 1:
            return [(me.slot(z=z), around) for z in zs]
        turns = [lax.rem(me.z + k, me.sz) for k in range(me.sz)]
        found = []
        for z in turns:
            even = lax.rem(z, 2) == 0
            if stage == 2:
                for y in ys:
                    found.append((me.slot(z=z, y=y), [(me.device(x=p), even) for p in xs] + [(me.twin, None)]))
                for x in xs:
                    found.append(
                        (me.slot(z=z, x=x), [(me.device(y=p), jnp.logical_not(even)) for p in ys] + [(me.twin, None)])
                    )
            else:
                for y in ys:
                    for x in xs:
                        found.append((me.slot(z=z, x=x, y=y), [(me.twin, None)]))
        return found

    def copies(self, a, stage):
        index = sum(len(to) for earlier in self.steps[a][:stage] for _, to in earlier)
        found = []
        for slot, to in self.steps[a][stage]:
            at = self.me.slot() if slot is None else slot
            source = self.ins[a] if slot is None else self.outs[a].at[at]
            group = []
            for device, when in to:
                group.append(
                    (remote(source, self.outs[a].at[at], self.send_sem.at[a, index], self.recv_sem.at[a, at], device), when)
                )
                index += 1
            found.append((slot, group))
        return found

    def arrived(self, a, slot):
        block = self.outs[a].at[slot]
        remote(block, block, self.send_sem.at[a, 0], self.recv_sem.at[a, slot], self.me.twin).wait_recv()

    def own(self, a):
        return pltpu.make_async_copy(self.ins[a], self.outs[a].at[self.me.slot()], self.local_sem.at[a])

    def run(self, stage):
        for a in range(len(self.ins)):
            if stage == 0:
                self.own(a).start()
            for slot, group in self.copies(a, stage):
                if slot is not None:
                    self.arrived(a, slot)
                for copy, when in group:
                    if when is None:
                        copy.start()
                    else:
                        pl.when(when)(copy.start)

    def finish(self):
        me = self.me
        for a in range(len(self.ins)):
            for x in range(me.sx):
                for seq in range(me.seqs):
                    self.arrived(a, (x * CORES + 1 - me.core) * me.seqs + seq)
            self.own(a).wait()
            for stage in range(4):
                for _, group in self.copies(a, stage):
                    for copy, when in group:
                        if when is None:
                            copy.wait_send()
                        else:
                            pl.when(when)(copy.wait_send)


def gather_semaphores(arrays):
    devices = lax.axis_size(AXES)
    return [
        pltpu.SemaphoreType.DMA((arrays,)),
        pltpu.SemaphoreType.DMA((arrays, 3 * devices)),
        pltpu.SemaphoreType.DMA((arrays, devices)),
    ]


class Exchange:
    def __init__(self, reverse, group, state, through, landed, out, parts, factors, ready, sems):
        self.reverse, self.group = reverse, group
        self.state, self.through, self.landed, self.out = state, through, landed, out
        self.parts, self.factors, self.ready, self.sems = parts, factors, ready, sems
        self.size, self.mine = lax.axis_size("seq"), lax.axis_index("seq")

    def copy(self, source, target, kind, index_out, index_in, peer):
        return remote(source, target, self.sems.at[kind, index_out], self.sems.at[kind + 1, index_in], {"seq": peer})

    def first(self):
        found = []
        for k in range(1, self.size):
            peer = lax.rem(self.mine + k, self.size)
            found.append(self.copy(self.through, self.factors.at[self.mine], 2, k, self.mine, peer))
            found.append(self.copy(self.state.at[peer], self.parts.at[self.mine], 0, k, self.mine, peer))
        return found

    def result(self, j):
        return self.copy(self.ready.at[j], self.out.at[self.mine], 4, j, self.mine, j)

    def start(self):
        greet([{"seq": lax.rem(self.mine + k, self.size)} for k in range(1, self.size)])
        for copy in self.first():
            copy.start()
        self.parts[self.mine] = self.state[self.mine]
        self.factors[self.mine] = self.through[...]

    def middle(self):
        group = self.group()
        heads = group.shape[0]
        total = jnp.zeros(self.state.shape[1:], F32)
        for k in range(self.size):
            j = self.size - 1 - k if self.reverse else k
            self.ready[j] = total.astype(LOW)

            @pl.when(self.mine != j)
            def _(j=j):
                self.result(j).start()
                self.copy(self.through, self.factors.at[j], 2, 0, j, j).wait_recv()
                self.copy(self.state.at[0], self.parts.at[j], 0, 0, j, j).wait_recv()

            factor = spread(self.factors[j][:, :heads], group)
            total = factor[0:1] * total + self.parts[j].astype(F32)
        self.out[self.mine] = self.ready[self.mine]

    def finish(self):
        for k in range(1, self.size):
            j = lax.rem(self.mine + k, self.size)
            self.copy(self.ready.at[j], self.out.at[j], 4, j, j, j).wait_recv()
        self.landed[...] = self.out[...]
        for copy in self.first():
            copy.wait_send()
        for j in range(self.size):
            pl.when(self.mine != j)(self.result(j).wait_send)


def exchange_scratch(pieces):
    size = pieces[0]
    return [
        pltpu.VMEM(pieces, LOW), pltpu.VMEM(pieces, LOW), pltpu.VMEM((size, 8, 128), F32), pltpu.VMEM(pieces, LOW),
        pltpu.SemaphoreType.DMA((6, size)),
    ]


def add_slots(target, first, source, pieces):
    def step(i, _):
        at = first + i
        target[at] = (target[at].astype(F32) + source[i].astype(F32)).astype(target.dtype)
        return 0

    lax.fori_loop(0, pieces, step, 0)


class Scatter:
    def __init__(self, me, sources, bufs, send_sem, recv_sem):
        self.me, self.sources, self.bufs = me, sources, bufs
        self.send_sem, self.recv_sem = send_sem, recv_sem
        self.order = [lax.rem(me.x + k, me.sx) for k in range(1, me.sx + 1)]
        self.even, self.odd = range(0, me.sz, 2), range(1, me.sz, 2)
        sx, sy, sz = me.sx, me.sy, me.sz
        self.base = [0, sx]
        for more in ((sx - 1) * sz, (sy - 1) * sx * sz, (sy - 1) * sz, (sx - 1) * sz):
            self.base.append(self.base[-1] + more)

    def plan(self, a, stage):
        me, base = self.me, self.base
        sx, sy, sz = me.sx, me.sy, me.sz
        twin_buf, total, from_x, from_y, from_y2, from_x2, from_z = self.bufs[a]
        xs, ys, zs = me.peers("x"), me.peers("y"), me.peers("z")
        found = []
        if stage == 0:
            for x in self.order:
                found.append((self.sources[a](x), twin_buf.at[x], x, me.twin))
        if stage == 1:
            for k, x in xs:
                for z in self.even:
                    found.append(
                        (
                            total.at[x, pl.ds(z * sy, sy)], from_x.at[k - 1, z], base[1] + (k - 1) * sz + z,
                            me.device(x=x),
                        )
                    )
            for k, y in ys:
                for z in self.odd:
                    for x in range(sx):
                        found.append(
                            (
                                total.at[x, z * sy + y], from_y.at[k - 1, x, z], base[2] + ((k - 1) * sx + x) * sz + z,
                                me.device(y=y),
                            )
                        )
        if stage == 2:
            for z in self.even:
                for k, y in ys:
                    found.append(
                        (total.at[me.x, z * sy + y], from_y2.at[k - 1, z], base[3] + (k - 1) * sz + z, me.device(y=y))
                    )
            for z in self.odd:
                for k, x in xs:
                    found.append(
                        (total.at[x, z * sy + me.y], from_x2.at[k - 1, z], base[4] + (k - 1) * sz + z, me.device(x=x))
                    )
        if stage == 3:
            for k, z in zs:
                found.append((total.at[me.x, z * sy + me.y], from_z.at[k - 1], base[5] + k - 1, me.device(z=z)))
        return found

    def copies(self, a, stage):
        me = self.me
        sx, sy = me.sx, me.sy
        ne, no = len(self.even), len(self.odd)
        counts = [sx, (sx - 1) * ne + (sy - 1) * no * sx, ne * (sy - 1) + no * (sx - 1)]
        index = sum(counts[:stage])
        return [
            remote(source, target, self.send_sem.at[a, index + i], self.recv_sem.at[a, arrival], device)
            for i, (source, target, arrival, device) in enumerate(self.plan(a, stage))
        ]

    def arrived(self, a, target, arrival):
        remote(target, target, self.send_sem.at[a, 0], self.recv_sem.at[a, arrival], self.me.twin).wait_recv()

    def send(self, a, stage):
        for copy in self.copies(a, stage):
            copy.start()

    def absorb(self, a, stage):
        me, base = self.me, self.base
        sx, sy, sz = me.sx, me.sy, me.sz
        twin_buf, total, from_x, from_y, from_y2, from_x2, from_z = self.bufs[a]
        if stage == 0:
            for x in self.order:
                self.arrived(a, twin_buf.at[x], x)
                add_slots(total.at[x], 0, twin_buf.at[x], me.seqs)
        if stage == 1:
            for k in range(1, sx):
                for z in self.even:
                    self.arrived(a, from_x.at[k - 1, z], base[1] + (k - 1) * sz + z)
                    add_slots(total.at[me.x], z * sy, from_x.at[k - 1, z], sy)
            for k in range(1, sy):
                for z in self.odd:
                    for x in range(sx):
                        self.arrived(a, from_y.at[k - 1, x, z], base[2] + ((k - 1) * sx + x) * sz + z)
                        add_slots(total.at[x], z * sy + me.y, from_y.at[k - 1, x, pl.ds(z, 1)], 1)
        if stage == 2:
            for z in range(sz):
                many, source, first = (sy, from_y2, base[3]) if z % 2 == 0 else (sx, from_x2, base[4])
                for k in range(1, many):
                    self.arrived(a, source.at[k - 1, z], first + (k - 1) * sz + z)
                    add_slots(total.at[me.x], z * sy + me.y, source.at[k - 1, pl.ds(z, 1)], 1)

    def result(self, a):
        me = self.me
        total, from_z = self.bufs[a][1], self.bufs[a][6]
        result = total[me.x, me.z * me.sy + me.y].astype(F32)
        for k in range(1, me.sz):
            self.arrived(a, from_z.at[k - 1], self.base[5] + k - 1)
            result = result + from_z[k - 1].astype(F32)
        return result

    def settle(self):
        for a in range(len(self.sources)):
            for stage in range(4):
                for copy in self.copies(a, stage):
                    copy.wait_send()


SCATTER_BUFFERS = 7


def scatter_scratch(ones, dtype=LOW):
    rows, seqs = lax.axis_size("row"), lax.axis_size("seq")
    sx, sz, sy = rows // CORES, DEPTH, seqs // DEPTH
    scratch = []
    for one in ones:
        for lead in ((sx, seqs), (sx, seqs), (sx - 1, sz, sy), (sy - 1, sx, sz), (sy - 1, sz), (sx - 1, sz), (sz - 1,)):
            scratch.append(pltpu.VMEM(lead + tuple(one), dtype))
    arrivals = sx + (sx - 1) * sz + (sy - 1) * sx * sz + (sy - 1) * sz + (sx - 1) * sz + sz - 1
    return scratch + [
        pltpu.SemaphoreType.DMA((len(ones), arrivals)),
        pltpu.SemaphoreType.DMA((len(ones), arrivals)),
    ]


def at_stage(stage, stages, act):
    count = pl.num_programs(0)
    pl.when(pl.program_id(0) == stage * count // stages)(act)


def weights_kernel(in_proj, small, hid, proj_o, small_o, halo_o, halo_buf, halo_sem, local_sem, send_sem, recv_sem):
    me = Place()
    greet(me.around() + [me.along(1), me.along(-1)])
    last = hid.at[pl.ds(hid.shape[0] - HALO, HALO)]
    halo = remote(last, halo_buf, halo_sem.at[0], halo_sem.at[1], me.along(1))
    halo.start()
    gather = Gather(me, [in_proj, small], [proj_o, small_o], local_sem, send_sem, recv_sem)
    for stage in range(4):
        gather.run(stage)
    gather.finish()
    halo.wait()
    halo_o[...] = jnp.where(me.seq > 0, halo_buf[...].astype(F32), 0.0).astype(LOW)


def project_kernel(
    sizes, info, hid, halo, proj, gain, rows, a_log, dt_bias, out_proj,
    normed_o, normed_halo_o, pre_o, maps_o, scaled_o, mixed_o, tail_o, step_o, run_o, run_t_o, sig_o,
    state_o, carry_o, final_o, through_o, out_all,
    ext, state, through, local_sem, send_sem, recv_sem,
):
    inner_width, channels, heads = sizes
    state_size = (channels - inner_width) // 2
    at = pl.program_id(0)
    me = Place()
    gather = Gather(me, [out_proj], [out_all], local_sem, send_sem, recv_sem)

    @pl.when(at == 0)
    def _():
        greet(me.around())

    for stage in range(4):
        at_stage(stage, 4, functools.partial(gather.run, stage))

    gain_row = gain[...]
    taps, offset = rows[0:4], rows[4:5]

    def norm(v):
        v = v.astype(F32)
        return (v * rms_rate(v) * gain_row).astype(LOW)

    weight = proj[:, inner_width : inner_width + channels]

    @pl.when(at == 0)
    def _():
        before = norm(halo[...])
        normed_halo_o[...] = before
        ext[0:EDGE] = nn(before, weight)[HALO - EDGE :]
        state[...] = jnp.zeros_like(state)
        through[...] = jnp.ones_like(through)

    labels = Labels(info, at)
    groups = head_groups(heads, inner_width)
    normed = norm(hid[...])
    normed_o[...] = normed
    mixed = nn(normed, weight)
    raw = nn(normed, proj[:, inner_width + channels :])
    ext[EDGE:] = mixed
    tail_o[0] = ext[0:EDGE]
    mixed_o[...] = mixed
    same = labels.same()
    total = offset + taps[3:4] * mixed
    for j in (1, 2, 3):
        total += taps[3 - j : 4 - j] * (same[:, j : j + 1] * ext[EDGE - j : EDGE - j + BLOCK])
    ext[0:EDGE] = mixed[BLOCK - EDGE :]
    pre_o[...] = total
    act = total * sigmoid(total)
    maps = act[:, inner_width:].astype(LOW)
    maps_o[...] = maps
    z = raw + dt_bias[...]
    step = jnp.maximum(z, 0.0) + log1p_of(jnp.exp(-jnp.abs(z)))
    log_decay = step * (-LOG2E * jnp.exp(a_log[...]))
    run = nn(triangle(), log_decay, HIGHEST)
    step_o[...] = step
    run_o[...] = run
    sig_o[...] = sigmoid(z)
    wide = jnp.concatenate([run, jnp.zeros((BLOCK, 128 - heads), F32)], axis=1)
    run_t_o[0] = jnp.transpose(wide)[:heads]
    last = run[BLOCK - 1 :]
    tail = labels.keep() * jnp.exp2(last - run)
    scaled = spread(step, groups) * act[:, :inner_width]
    scaled_o[...] = scaled.astype(LOW)
    weighted = (spread(tail, groups) * scaled).astype(LOW)
    fresh = tn(maps[:, :state_size], weighted)
    state_o[0] = fresh
    factor = labels.flag()[:, :heads] * jnp.exp2(jnp.broadcast_to(last, (8, heads)))
    through[:, :heads] = through[:, :heads] * factor
    factor = spread(factor, groups)
    carry_o[0] = factor
    state[...] = factor[0:1] * state[...] + fresh

    @pl.when(at == pl.num_programs(0) - 1)
    def _():
        final_o[...] = state[...].astype(LOW)
        through_o[...] = through[...]
        gather.finish()


def inner_kernel(
    sizes, info, normed, proj, maps, scaled, run, run_t, final, through, gate_o, inner_o, inbound_o, *scratch
):
    inner_width, channels, heads = sizes
    state_size = (channels - inner_width) // 2
    head_size = inner_width // heads
    at = pl.program_id(0)
    exchange = Exchange(False, lambda: head_groups(heads, inner_width), final, through, inbound_o, *scratch)
    pl.when(at == 0)(exchange.start)
    pl.when(at == pl.num_programs(0) // 2)(exchange.middle)
    labels = Labels(info, at)
    gate_o[...] = nn(normed[...], proj[...])
    in_map = maps[:, :state_size]
    out_map = maps[:, state_size:]
    q_at = lax.broadcasted_iota(jnp.int32, (BLOCK, BLOCK), 0)
    s_at = lax.broadcasted_iota(jnp.int32, (BLOCK, BLOCK), 1)
    inside = (q_at >= s_at) & (labels.column() == labels.row())
    scores = jnp.where(inside, nt(out_map, in_map), 0.0)
    lane = lax.broadcasted_iota(jnp.int32, (BLOCK, 2 * head_size), 1)
    run_q = run[...]
    for pair in range(heads // 2):
        span = slice(pair * 2 * head_size, (pair + 1) * 2 * head_size)
        values = scaled[:, span]
        parts = []
        for h in (2 * pair, 2 * pair + 1):
            decay = jnp.exp2(jnp.minimum(run_q[:, h : h + 1] - run_t[0, h : h + 1], 0.0))
            parts.append(nn((scores * decay).astype(LOW), values))
        inner_o[:, span] = jnp.where(lane < head_size, parts[0], parts[1])
    pl.when(at == pl.num_programs(0) - 1)(exchange.finish)


def gate_kernel(
    sizes, info, hid, cot, gate, inner, pre, maps, run, state, carry, inbound, out_proj, gain, skip,
    block_o, gated_o, masked_o, back_o, enter_back_o, gate_back_o, row_o, out_back_o, enter_o, leaving_o, gain_o, skip_o,
    now, leaving, through,
):
    inner_width, channels, heads = sizes
    state_size = (channels - inner_width) // 2
    at = pl.program_id(0)
    labels = Labels(info, at)
    groups = head_groups(heads, inner_width)

    @pl.when(at == 0)
    def _():
        now[...] = inbound[...].astype(F32)
        leaving[...] = jnp.zeros_like(leaving)
        through[...] = jnp.ones_like(through)
        gain_o[...] = jnp.zeros_like(gain_o)
        skip_o[...] = jnp.zeros_like(skip_o)

    values = pre[...]
    values = values * sigmoid(values)
    out_map = maps[:, state_size:]
    entry = spread(labels.entry() * jnp.exp2(run[...]), groups)
    entering = now[...]
    enter_o[0] = entering
    enter_high, enter_rest = halves(entering)
    scanned = inner[...] + entry * nn(out_map, enter_high)
    factor = carry[0, 0:1]
    now[...] = factor * entering + state[0]
    mixer = scanned + spread(jnp.broadcast_to(skip[...], (8, heads)), groups)[0:1] * values
    g = gate[...]
    sg = sigmoid(g)
    si = g * sg
    gated = mixer * si
    rate = rms_rate(gated)
    unit = gated * rate
    gain_row = gain[...]
    gated_low = (unit * gain_row).astype(LOW)
    gated_o[...] = gated_low
    valid = labels.valid()
    branch = nn(gated_low, out_proj[...])
    block_o[...] = (valid * (hid[...].astype(F32) + branch)).astype(LOW)
    masked = (valid * cot[...].astype(F32)).astype(LOW)
    masked_o[...] = masked
    back = nt(masked, out_proj[...])
    product = back * unit
    gain_o[...] += jnp.sum(product, axis=0, keepdims=True)
    mean = jnp.mean(product * gain_row, axis=-1, keepdims=True)
    gated_back = rate * (back * gain_row - unit * mean)
    mixer_back = gated_back * si
    gate_back_o[...] = (gated_back * mixer * (sg + si * (1.0 - sg))).astype(LOW)
    skip_o[...] += jnp.sum(mixer_back * values, axis=0, keepdims=True)
    back_low = mixer_back.astype(LOW)
    back_o[...] = back_low
    row_o[...] = head_sums(back_low.astype(F32) * scanned, groups)
    back_high, back_rest = halves(entry * mixer_back)
    enter_back_o[...] = back_high
    out_back_o[...] = nt(back_high, enter_high) + nt(back_rest, enter_high) + nt(back_high, enter_rest)
    leaving[...] += through[0:1] * tn(out_map, back_high)
    through[...] = through[...] * factor

    @pl.when(at == pl.num_programs(0) - 1)
    def _():
        leaving_o[...] = leaving[...].astype(LOW)


def inner_back_kernel(
    sizes, info, maps, scaled, back, run, run_t, gated, masked, normed, gate_back, leaving, through,
    values_o, maps_o, col_o, out_grad_o, gate_grad_o, onward_o, *scratch
):
    inner_width, channels, heads = sizes
    state_size = (channels - inner_width) // 2
    head_size = inner_width // heads
    at = pl.program_id(0)
    exchange = Exchange(True, lambda: head_groups(heads, inner_width), leaving, through, onward_o, *scratch)
    pl.when(at == 0)(exchange.start)
    pl.when(at == pl.num_programs(0) // 2)(exchange.middle)
    out_grad_o[...] = tn(gated[...], masked[...]).astype(LOW)
    gate_grad_o[...] = tn(normed[...], gate_back[...]).astype(LOW)
    labels = Labels(info, at)
    in_map = maps[:, :state_size]
    out_map = maps[:, state_size:]
    s_at = lax.broadcasted_iota(jnp.int32, (BLOCK, BLOCK), 0)
    q_at = lax.broadcasted_iota(jnp.int32, (BLOCK, BLOCK), 1)
    inside = (q_at >= s_at) & (labels.column() == labels.row())
    scores = jnp.where(inside, nt(in_map, out_map), 0.0)
    lane = lax.broadcasted_iota(jnp.int32, (BLOCK, 2 * head_size), 1)
    run_s = run[...]
    total = jnp.zeros((BLOCK, BLOCK), F32)
    for pair in range(heads // 2):
        span = slice(pair * 2 * head_size, (pair + 1) * 2 * head_size)
        values = scaled[:, span]
        grad = back[:, span]
        parts = []
        for h in (2 * pair, 2 * pair + 1):
            mine = (lane < head_size) == (h % 2 == 0)
            decay = jnp.exp2(jnp.minimum(run_t[0, h : h + 1] - run_s[:, h : h + 1], 0.0))
            parts.append(nn((scores * decay).astype(LOW), grad))
            total += decay * nt(jnp.where(mine, values, jnp.zeros_like(values)), grad)
        values_o[:, span] = jnp.where(lane < head_size, parts[0], parts[1])
    total = jnp.where(inside, total, 0.0).astype(LOW)
    maps_o[:, :state_size] = nn(total, out_map)
    maps_o[:, state_size:] = tn(total, in_map)
    col_o[...] = head_sums(values_o[...] * scaled[...].astype(F32), head_groups(heads, inner_width))
    pl.when(at == pl.num_programs(0) - 1)(exchange.finish)


def finish_kernel(
    sizes, info, hid, halo, masked, pre, maps, scaled, back, enter_back, values_in, maps_in, out_in, col_in, row_in,
    step, run, sig, gate_back, enter, carry, onward, mixed, mixed_tail, proj, gain, rows, a_log, skip, inner_gain_sum,
    skip_sum, out_grad, gate_grad,
    late_o, late_halo_o, hid_o, last_o, halo_hid_o, sums_o, out_sum_o, gate_sum_o,
    state, ext, near, local_sem, *scratch
):
    inner_width, channels, heads = sizes
    state_size = (channels - inner_width) // 2
    at = pl.num_programs(0) - 1 - pl.program_id(0)
    first_step = pl.program_id(0) == 0
    last_step = pl.program_id(0) == pl.num_programs(0) - 1

    me = Place()
    grads = [out_grad, gate_grad]
    bufs = [scratch[SCATTER_BUFFERS * a : SCATTER_BUFFERS * (a + 1)] for a in range(2)]

    def part(a, x, core):
        return grads[a].at[pl.ds((x * CORES + core) * me.seqs, me.seqs)]

    scatter = Scatter(
        me, [functools.partial(part, a, core=1 - me.core) for a in range(2)], bufs, *scratch[2 * SCATTER_BUFFERS :]
    )

    def own(a, x):
        return pltpu.make_async_copy(part(a, x, me.core), bufs[a][1].at[x], local_sem.at[a, x])

    def stage_0():
        greet(me.around())
        for a in range(2):
            scatter.send(a, 0)
            for x in range(me.sx):
                own(a, x).start()

    def stage_1():
        for a in range(2):
            for x in range(me.sx):
                own(a, x).wait()
            scatter.absorb(a, 0)
            scatter.send(a, 1)

    def stage_2():
        for a in range(2):
            scatter.absorb(a, 1)
            scatter.send(a, 2)

    def stage_3():
        for a in range(2):
            scatter.absorb(a, 2)
            scatter.send(a, 3)

    for stage, act in enumerate((stage_0, stage_1, stage_2, stage_3)):
        at_stage(stage, 4, act)

    @pl.when(first_step)
    def _():
        state[...] = onward[...].astype(F32)
        ext[0:EDGE] = jnp.zeros((EDGE, channels), F32)
        ext[EDGE + BLOCK :] = jnp.zeros((EDGE, channels), F32)
        sums_o[...] = jnp.zeros_like(sums_o)

    labels = Labels(info, at)
    group = head_groups(heads, inner_width)
    taps = rows[0:4]
    u = pre[...]
    sg = sigmoid(u)
    act = u * sg
    slope = sg + act * (1.0 - sg)
    values = act[:, :inner_width]
    in_map = maps[:, :state_size]
    out_map = maps[:, state_size:]
    run_q = run[...]
    steps = step[...]
    tail = spread(labels.keep() * jnp.exp2(run_q[BLOCK - 1 :] - run_q), group)
    grad = back[...].astype(F32)
    scaled_f = scaled[...].astype(F32)
    state_low = state[...].astype(LOW)
    from_tail = tail * nn(in_map, state_low)
    col_tail = head_sums(scaled_f * from_tail, group)
    scaled_back = values_in[...] + from_tail
    step_back = head_sums(values * scaled_back, group)
    skip_row = spread(jnp.broadcast_to(skip[...], (8, heads)), group)[0:1]
    values_back = spread(steps, group) * scaled_back + skip_row * grad
    in_back = maps_in[:, :state_size] + nt((tail * scaled_f).astype(LOW), state_low)
    out_back = maps_in[:, state_size:] + out_in[...]
    factor = carry[0, 0:1]
    shared = jnp.sum(enter[0] * state[...], axis=0, keepdims=True) * factor
    shared = head_sums(jnp.broadcast_to(shared, (8, inner_width)), group)[0:1]
    state[...] = factor * state[...] + tn(out_map, enter_back[...])
    order = triangle()
    decay_back = (
        tn(order, row_in[...] - col_in[...], HIGHEST) + nn(order, col_tail, HIGHEST) - col_tail + shared
    )
    rate_row = jnp.exp(a_log[...])
    sums_o[7:8, 0:heads] += jnp.sum(decay_back * steps, axis=0, keepdims=True) * -rate_row
    raw_back = (step_back - rate_row * decay_back) * sig[...]
    sums_o[7:8, 128 : 128 + heads] += jnp.sum(raw_back, axis=0, keepdims=True)
    raw_low = raw_back.astype(LOW)
    late_o[:, channels:] = raw_low
    ext[EDGE : EDGE + BLOCK, :inner_width] = values_back * slope[:, :inner_width]
    ext[EDGE : EDGE + BLOCK, inner_width : inner_width + state_size] = (
        in_back * slope[:, inner_width : inner_width + state_size]
    )
    ext[EDGE : EDGE + BLOCK, inner_width + state_size :] = out_back * slope[:, inner_width + state_size :]
    pre_back = ext[EDGE : EDGE + BLOCK]
    near[0:EDGE] = mixed_tail[0]
    near[EDGE:] = mixed[...]
    sums_o[4:5] += jnp.sum(pre_back, axis=0, keepdims=True)
    sums_o[3:4] += jnp.sum(pre_back * near[EDGE:], axis=0, keepdims=True)
    total = taps[3:4] * pre_back
    same = Labels(info, at, BLOCK + EDGE).same()
    for j in (1, 2, 3):
        sums_o[3 - j : 4 - j] += jnp.sum(
            pre_back * (same[:BLOCK, j : j + 1] * near[EDGE - j : EDGE - j + BLOCK]), axis=0, keepdims=True
        )
        total += taps[3 - j : 4 - j] * (same[j : j + BLOCK, j : j + 1] * ext[EDGE + j : EDGE + j + BLOCK])
    mixed_low = total.astype(LOW)
    late_o[:, :channels] = mixed_low
    ext[EDGE + BLOCK :] = ext[EDGE : 2 * EDGE]
    gain_row = gain[...]
    weight = proj[:, inner_width : inner_width + channels]

    def norm_back(normed_back, v):
        rate = rms_rate(v)
        unit = v * rate
        product = normed_back * unit
        mean = jnp.mean(product * gain_row, axis=-1, keepdims=True)
        sums_o[6:7, : v.shape[1]] += jnp.sum(product, axis=0, keepdims=True)
        return rate * (normed_back * gain_row - unit * mean)

    normed_back = (
        nt(gate_back[...], proj[:, :inner_width])
        + nt(mixed_low, weight)
        + nt(raw_low, proj[:, inner_width + channels :])
    )
    result = masked[...].astype(F32) + norm_back(normed_back, hid[...].astype(F32))
    hid_o[...] = result.astype(LOW)

    @pl.when(first_step)
    def _():
        last_o[...] = result[BLOCK - HALO :]

    @pl.when(last_step)
    def _():
        padded = jnp.concatenate([jnp.zeros((EDGE, 8), F32), same[:EDGE]], axis=0)
        edge = jnp.zeros((EDGE, channels), F32)
        for j in (1, 2, 3):
            edge += taps[3 - j : 4 - j] * (padded[j : j + EDGE, j : j + 1] * ext[j : j + EDGE])
        edge_low = jnp.concatenate([jnp.zeros((HALO - EDGE, channels), F32), edge], axis=0).astype(LOW)
        late_halo_o[:, :channels] = edge_low
        late_halo_o[:, channels:] = jnp.zeros((HALO, heads), LOW)
        halo_hid_o[...] = norm_back(nt(edge_low, weight), halo[...].astype(F32))
        sums_o[5:6, :inner_width] = inner_gain_sum[...]
        skip_total = head_sums(jnp.broadcast_to(skip_sum[...], (8, inner_width)), group)
        sums_o[7:8, 256 : 256 + heads] = skip_total[0:1]
        for a, out in enumerate((out_sum_o, gate_sum_o)):
            out[...] = scatter.result(a)
        scatter.settle()


def last_kernel(
    sizes, normed, normed_halo, late, late_halo, gate_sum, sums, halo_hid, last,
    proj_o, taps_o, offset_o, inner_gain_o, gain_o, a_log_o, dt_bias_o, skip_o, last_o,
    halo_buf, halo_sem, small_buf, small_sem, other, *scratch
):
    inner_width, channels, heads = sizes
    me = Place()
    bufs = scratch[:SCATTER_BUFFERS]
    scatter = Scatter(me, [lambda x: other.at[x]], [bufs], *scratch[SCATTER_BUFFERS:])
    greet(me.around() + [me.along(1), me.along(-1)])
    halo = remote(halo_hid, halo_buf, halo_sem.at[0], halo_sem.at[1], me.along(-1))
    halo.start()

    axes = [
        (CORES, me.core, [(1, 1 - me.core, me.twin)]),
        (me.sx, me.x, [(k, p, me.device(x=p)) for k, p in me.peers("x")]),
        (me.sy, me.y, [(k, p, me.device(y=p)) for k, p in me.peers("y")]),
        (me.sz, me.z, [(k, p, me.device(z=p)) for k, p in me.peers("z")]),
    ]

    def small_copies(stage):
        _, mine, peers = axes[stage]
        buf = small_buf.at[stage, mine]
        return [remote(buf, buf, small_sem.at[0, stage, k], small_sem.at[1, stage, mine], device) for k, _, device in peers]

    def small_send(stage, value):
        small_buf[stage, axes[stage][1]] = value
        for copy in small_copies(stage):
            copy.start()

    def small_take(stage):
        size, _, peers = axes[stage]
        for _, p, _ in peers:
            buf = small_buf.at[stage, p]
            remote(buf, buf, small_sem.at[0, stage, 0], small_sem.at[1, stage, p], me.twin).wait_recv()
        total = small_buf[stage, 0]
        for i in range(1, size):
            total = total + small_buf[stage, i]
        return total

    small_send(0, sums[...])

    own_rows = normed.shape[1] // me.count
    half = me.seqs * own_rows
    mine = bufs[1]
    starts = scatter.copies(0, 0)
    for x in range(me.sx):
        span = slice(2 * half * x, 2 * half * (x + 1))
        grad = tn(normed[:, span], late[...]) + tn(normed_halo[:, span], late_halo[...])
        first = me.core == 0
        here = jnp.where(first, grad[:half], grad[half:])
        there = jnp.where(first, grad[half:], grad[:half])
        for i in range(me.seqs):
            other[x, i] = there[i * own_rows : (i + 1) * own_rows].astype(LOW)
            mine[x, i] = here[i * own_rows : (i + 1) * own_rows].astype(LOW)
        for k in range(me.sx):
            pl.when(scatter.order[k] == x)(starts[k].start)
    value = small_take(0)
    small_send(1, value)
    scatter.absorb(0, 0)
    scatter.send(0, 1)
    value = small_take(1)
    small_send(2, value)
    scatter.absorb(0, 1)
    scatter.send(0, 2)
    value = small_take(2)
    small_send(3, value)
    scatter.absorb(0, 2)
    scatter.send(0, 3)
    total = small_take(3)
    mine_at = me.row * me.seqs + me.seq

    def own(v, size):
        width = v.shape[1]
        return pltpu.roll(v, lax.rem(width - mine_at * size, width), 1)[:, :size]

    taps_o[...] = own(total, taps_o.shape[1])[0:4]
    offset_o[...] = own(total, offset_o.shape[1])[4:5]
    inner_gain_o[...] = own(total, inner_gain_o.shape[1])[5:6]
    gain_o[...] = own(total, gain_o.shape[1])[6:7]
    a_log_o[...] = total[7:8, 0:heads]
    dt_bias_o[...] = total[7:8, 128 : 128 + heads]
    skip_o[...] = total[7:8, 256 : 256 + heads]
    halo.wait()
    last_o[...] = last[...] + jnp.where(me.seq < me.seqs - 1, halo_buf[...], 0.0)
    proj_o[:, :inner_width] = gate_sum[...]
    proj_o[:, inner_width:] = scatter.result(0)
    scatter.settle()
    for stage in range(4):
        for copy in small_copies(stage):
            copy.wait_send()


def struct(shape, dtype=F32):
    return jax.ShapeDtypeStruct(shape, dtype)


def run_kernel(kernel, name, count, ins, outs, scratch=(), flip=False, collective_id=None):
    def block(i):
        return count - 1 - i if flip else i

    def spec(array, kind):
        shape = array.shape
        zeros = (0,) * (len(shape) - 1)
        if kind == "any":
            return pl.BlockSpec(memory_space=pl.ANY)
        if kind == "scalar":
            return pl.BlockSpec(memory_space=pltpu.SMEM)
        if kind == "w":
            return pl.BlockSpec(shape, lambda i: (0,) + zeros)
        if kind == "once":
            return pl.BlockSpec(shape, lambda i: (0,) + zeros, pipeline_mode=pl.Buffered(1))
        if kind == "r":
            return pl.BlockSpec((BLOCK,) + shape[1:], lambda i: (block(i),) + zeros)
        if kind == "b":
            return pl.BlockSpec((1,) + shape[1:], lambda i: (block(i),) + zeros)
        if kind == "c":
            return pl.BlockSpec((shape[0], shape[1] // count), lambda i: (0, i))
        if kind == "part":
            return pl.BlockSpec((shape[0] // count, shape[1]), lambda i: (i, 0))
        if kind[0] == "r":
            return pl.BlockSpec((BLOCK, kind[1]), lambda i: (block(i), 0))
        return pl.BlockSpec(kind, lambda i: (0,) * len(kind))

    return pl.pallas_call(
        kernel,
        name=name,
        grid=(count,),
        in_specs=[spec(a, k) for a, k in ins],
        out_specs=[spec(a, k) for a, k in outs],
        out_shape=[a for a, _ in outs],
        scratch_shapes=list(scratch),
        compiler_params=pltpu.CompilerParams(
            dimension_semantics=("arbitrary",),
            vmem_limit_bytes=VMEM_BYTES,
            collective_id=collective_id,
            has_side_effects=collective_id is not None,
        ),
    )(*[a for a, _ in ins])


def body(
    hidden, lengths, cotangent, norm_gain, in_proj, conv_weight, conv_bias, a_log, dt_bias, skip_weight, inner_gain,
    out_proj,
):
    length, model = hidden.shape[1:]
    count = length // BLOCK
    heads = a_log.shape[0]
    devices = lax.axis_size(AXES)
    seqs = lax.axis_size("seq")
    inner_width = out_proj.shape[0] * devices
    channels = conv_weight.shape[1] * devices
    state_size = (channels - inner_width) // 2
    sizes = (inner_width, channels, heads)
    hid = hidden[0]
    cot = cotangent[0]
    width, part = conv_weight.shape
    own_rows, columns = in_proj.shape
    a_row, bias_row, skip_row = a_log[None], dt_bias[None], skip_weight[None]
    info = jnp.concatenate([lengths, (lax.axis_index("seq") * length).reshape(1, 1)], axis=1)

    def padded(v):
        v = v.astype(F32)
        return jnp.pad(v, ((0, 0), (0, part - v.shape[1])))

    small = jnp.concatenate(
        [conv_weight.astype(F32), padded(conv_bias[None]), padded(inner_gain[None]), padded(norm_gain[None])]
        + [jnp.zeros((8 - width - 3, part), F32)]
    )
    proj_all, small_all, halo = run_kernel(
        weights_kernel, "weights", 1,
        [(in_proj, "any"), (small, "any"), (hid, "any")],
        [
            (struct((devices,) + in_proj.shape, LOW), "any"), (struct((devices,) + small.shape), "any"),
            (struct((HALO, model), LOW), "w"),
        ],
        [pltpu.VMEM((HALO, model), LOW), pltpu.SemaphoreType.DMA((2,))] + gather_semaphores(2),
        collective_id=0,
    )
    proj_full = proj_all.reshape(model, columns)
    rows = jnp.moveaxis(small_all, 1, 0).reshape(8, channels)
    inner_gain_row = small_all[:, width + 1, : inner_gain.shape[0]].reshape(1, inner_width)
    gain_row = small_all[:, width + 2, :own_rows].reshape(1, model)

    token = struct((length, inner_width), LOW)
    (
        normed, normed_halo, pre, maps, scaled, mixed, mixed_tail, step, run, run_t, sig, state, carry, final_state,
        through, out_all,
    ) = run_kernel(
        functools.partial(project_kernel, sizes), "project", count,
        [
            (info, "scalar"), (hid, "r"), (halo, "w"), (proj_full, "once"), (gain_row, "w"), (rows, "w"), (a_row, "w"),
            (bias_row, "w"), (out_proj, "any"),
        ],
        [
            (struct((length, model), LOW), "r"), (struct((HALO, model), LOW), "w"),
            (struct((length, channels)), "r"), (struct((length, 2 * state_size), LOW), "r"),
            (token, "r"), (struct((length, channels)), "r"),
            (struct((count, EDGE, channels)), "b"), (struct((length, heads)), "r"), (struct((length, heads)), "r"),
            (struct((count, heads, BLOCK)), "b"), (struct((length, heads)), "r"),
            (struct((count, state_size, inner_width)), "b"), (struct((count, 8, inner_width)), "b"),
            (struct((state_size, inner_width), LOW), "w"), (struct((8, 128)), "w"),
            (struct((devices,) + out_proj.shape, LOW), "any"),
        ],
        [
            pltpu.VMEM((EDGE + BLOCK, channels), F32), pltpu.VMEM((state_size, inner_width), F32),
            pltpu.VMEM((8, 128), F32),
        ] + gather_semaphores(1),
        collective_id=1,
    )
    out_full = out_all.reshape(inner_width, model)
    pieces = (seqs, state_size // seqs, inner_width)
    gate, inner, inbound = run_kernel(
        functools.partial(inner_kernel, sizes), "inner", count,
        [
            (info, "scalar"), (normed, "r"), (proj_full, (model, inner_width)), (maps, "r"), (scaled, "r"), (run, "r"),
            (run_t, "b"), (final_state.reshape(pieces), "w"), (through, "w"),
        ],
        [
            (struct((length, inner_width)), "r"), (struct((length, inner_width)), "r"), (struct(pieces, LOW), "w"),
        ],
        exchange_scratch(pieces),
        collective_id=2,
    )
    (
        block_out, gated, masked, back, enter_back, gate_back, row_term, out_in, enter, leaving, inner_gain_sum, skip_sum,
    ) = run_kernel(
        functools.partial(gate_kernel, sizes), "gate", count,
        [
            (info, "scalar"), (hid, "r"), (cot, "r"), (gate, "r"), (inner, "r"), (pre, ("r", inner_width)), (maps, "r"),
            (run, "r"), (state, "b"), (carry, "b"), (inbound.reshape(state_size, inner_width), "w"), (out_full, "once"),
            (inner_gain_row, "w"), (skip_row, "w"),
        ],
        [
            (struct((length, model), LOW), "r"), (token, "r"), (struct((length, model), LOW), "r"), (token, "r"),
            (token, "r"), (token, "r"), (struct((length, heads)), "r"), (struct((length, state_size)), "r"),
            (struct((count, state_size, inner_width)), "b"), (struct((state_size, inner_width), LOW), "w"),
            (struct((1, inner_width)), "w"), (struct((1, inner_width)), "w"),
        ],
        [
            pltpu.VMEM((state_size, inner_width), F32), pltpu.VMEM((state_size, inner_width), F32),
            pltpu.VMEM((8, inner_width), F32),
        ],
    )
    values_in, maps_in, col_in, out_grad, gate_grad, onward = run_kernel(
        functools.partial(inner_back_kernel, sizes), "inner_back", count,
        [
            (info, "scalar"), (maps, "r"), (scaled, "r"), (back, "r"), (run, "r"), (run_t, "b"), (gated, "c"),
            (masked, "w"), (normed, "w"), (gate_back, "c"), (leaving.reshape(pieces), "w"), (through, "w"),
        ],
        [
            (struct((length, inner_width)), "r"), (struct((length, 2 * state_size)), "r"),
            (struct((length, heads)), "r"), (struct((inner_width, model), LOW), "part"),
            (struct((model, inner_width), LOW), "c"), (struct(pieces, LOW), "w"),
        ],
        exchange_scratch(pieces),
        collective_id=3,
    )
    gate_one = (own_rows, inner_width)
    late_width = columns - inner_width
    late, late_halo, hid_grad, last_rows, halo_hid, sums, out_sum, gate_sum = run_kernel(
        functools.partial(finish_kernel, sizes), "finish", count,
        [
            (info, "scalar"), (hid, "r"), (halo, "w"), (masked, "r"), (pre, "r"), (maps, "r"), (scaled, "r"),
            (back, "r"), (enter_back, "r"), (values_in, "r"), (maps_in, "r"), (out_in, "r"), (col_in, "r"),
            (row_term, "r"), (step, "r"), (run, "r"), (sig, "r"), (gate_back, "r"), (enter, "b"), (carry, "b"),
            (onward.reshape(state_size, inner_width), "w"), (mixed, "r"), (mixed_tail, "b"), (proj_full, "once"),
            (gain_row, "w"), (rows, "w"), (a_row, "w"), (skip_row, "w"), (inner_gain_sum, "w"), (skip_sum, "w"),
            (out_grad.reshape(devices, -1, model), "any"), (gate_grad.reshape(devices, -1, inner_width), "any"),
        ],
        [
            (struct((length, late_width), LOW), "r"), (struct((HALO, late_width), LOW), "w"),
            (struct((length, model), LOW), "r"), (struct((HALO, model)), "w"), (struct((HALO, model)), "w"),
            (struct((8, channels)), "w"), (struct(out_proj.shape), "w"), (struct(gate_one), "w"),
        ],
        [
            pltpu.VMEM((state_size, inner_width), F32), pltpu.VMEM((2 * EDGE + BLOCK, channels), F32),
            pltpu.VMEM((EDGE + BLOCK, channels), F32), pltpu.SemaphoreType.DMA((2, lax.axis_size("row") // CORES)),
        ] + scatter_scratch([out_proj.shape, gate_one]),
        flip=True,
        collective_id=4,
    )
    late_one = (own_rows, late_width)
    most = max(CORES, lax.axis_size("row") // CORES, DEPTH, seqs // DEPTH)
    sx = lax.axis_size("row") // CORES
    row = struct((1, heads))
    proj_sum, taps_sum, offset_sum, inner_sum, gain_sum, a_log_sum, dt_bias_sum, skip_total, last_rows = run_kernel(
        functools.partial(last_kernel, sizes), "last", 1,
        [
            (normed, "once"), (normed_halo, "w"), (late, "once"), (late_halo, "w"), (gate_sum, "w"), (sums, "w"),
            (halo_hid, "w"), (last_rows, "w"),
        ],
        [
            (struct(in_proj.shape), "w"), (struct((width, part)), "w"), (struct((1, part)), "w"),
            (struct((1, inner_gain.shape[0])), "w"), (struct((1, own_rows)), "w"), (row, "w"), (row, "w"), (row, "w"),
            (struct((HALO, model)), "w"),
        ],
        [
            pltpu.VMEM((HALO, model), F32), pltpu.SemaphoreType.DMA((2,)), pltpu.VMEM((4, most, 8, channels), F32),
            pltpu.SemaphoreType.DMA((2, 4, most)), pltpu.VMEM((sx, seqs) + late_one, LOW),
        ] + scatter_scratch([late_one]),
        collective_id=5,
    )
    hidden_grad = jnp.concatenate([hid_grad[: length - HALO], last_rows.astype(LOW)])
    return (
        block_out[None], hidden_grad[None], gain_sum[0], proj_sum, taps_sum, offset_sum[0], a_log_sum[0], dt_bias_sum[0],
        skip_total[0], inner_sum[0], out_sum,
    )


def solution(mesh):
    weights = P(AXES)
    tokens = P("row", "seq", None)
    rows = P(AXES, None)
    return jax.shard_map(
        body,
        mesh=mesh,
        in_specs=(
            tokens, P("row", None), tokens, weights, rows, P(None, AXES), weights, P(), P(), P(), weights, rows,
        ),
        out_specs=(tokens, tokens, weights, rows, P(None, AXES), weights, P(), P(), P(), weights, rows),
        check_vma=False,
    )
```

time: 877 us -> 267 us (0.30); the launches traced: 868 us -> 267 us
  Pallas kernels: 0 us -> 249 us
  matrix products: 225 us -> 0 us
  other arithmetic: 183 us -> 3.82 us
  blocking collectives: 170 us -> 0 us
  local copies, waits for them, and re-layouts: 148 us -> 12.9 us
  waiting for transfers between devices: 121 us -> 0 us
  between operations: 16.2 us -> 0.82 us
    pallas_call x0 -> x7, Pallas kernels: none -> 249 us  [run_kernel(): pl.pallas_call(kernel, name=name, grid=(count,), in_specs=[spec(a, k) for...]
    dot_general x24 -> x0, matrix products: 225 us -> none  [the longest x3 101 us: block_parts(): inner = jnp.einsum('rkhqs,rkshp->rkqhp', mixing, blocked, precision=HIGHEST)]
    all_gather x2 -> x0, blocking collectives: 85.7 us -> none  [the longest x1 66.7 us: body(): lax.all_gather(conv_weight, ('row', 'seq'), axis=1, tiled=True)]
    unnamed x2 -> x0, blocking collectives: 83.9 us -> none
    unnamed x7 -> x0, waiting for transfers between devices: 73.8 us -> none
    reduce_sum x19 -> x0, other arithmetic: 48.1 us -> none  [the longest x1 12.8 us: causal_conv(): jnp.where(same, padded[:, index:index + length_value], 0.0) * kernel[index]]
    all_gather x4 -> x0, waiting for transfers between devices: 46.7 us -> none  [the longest x2 46.7 us: entering_2(): everything = jax.tree.map(lambda part: lax.all_gather(part, axis), array)]
    reshape x8 -> x1, local copies, waits for them, and re-layouts: 42.6 us -> 0.74 us  [body(): rows = jnp.moveaxis(small_all, 1, 0).reshape(8, channels)]
  transfers between devices with their start and end apart: 8 -> 0, of which waited for: 3 -> 0; matrix products, arithmetic and copies ran while one was open for 51% -> 0% of each run, Pallas kernels for 0% -> 0%
where the time goes in v1:
time: 267 us
  Pallas kernels  249 us (93%)
  local copies, waits for them, and re-layouts  12.9 us (5%)
  other arithmetic  3.82 us (1%)
    pallas_call x7, Pallas kernels, run_kernel(): pl.pallas_call(kernel, name=name, grid=(count,), in_specs=[spec(a, k) for...  249 us

profile of v1, /device:TPU:0, one launch (start us, length us, event | category | flops | bytes accessed | tf_op | source)
XLA Modules:
  0.0 266.5 jit_solution(13178195729835043519)
XLA Ops:
  0.6 1.2 pad_add_fusion.info
  1.9 0.7 bitcast_convert_fusion
  2.5 0.7 pad_convert_fusion
  3.2 1.3 concatenate.10.small
  4.5 41.1 %weights.1 = (bf16[32,24,3352]{2,1,0:T(8,128)(2,1)}, f32[32,8,56]{2,1,0:T(8,128)}, bf16[16,768]{1,0:T(8,128)(2,1)}) custom-call(bf16[24,3352]{1,0:T(8,128)(2,1)} %in_proj.1, f32[8,56]{1,0:T(8,128)} %concatenate.10.small, bf16[1024,768]{1,0:T(8,128)(2,1)} %bitcast.32), custom_call_target="tpu_custom_call" | custom-call | tf_op jit(solution)/shard_map/weights/pallas_call | solution.py:1000
  45.6 1.0 slice_reduce_fusion
  46.6 0.7 reshape_squeeze.7.gain
  47.3 1.0 slice_reduce_fusion.1
  48.2 0.7 reshape_squeeze.6.gain
  48.9 0.9 copy.24
  49.8 0.7 reshape.60.rows
  50.6 34.2 %project.1 = (bf16[1024,768]{1,0:T(8,128)(2,1)}, bf16[16,768]{1,0:T(8,128)(2,1)}, f32[1024,1792]{1,0:T(8,128)}, bf16[1024,256]{1,0:T(8,128)(2,1)}, bf16[1024,153...) custom-call(s32[1,5]{1,0:T(1,128)} %pad_add_fusion.info, ...), custom_call_target="tpu_custom_call" | custom-call | tf_op jit(solution)/shard_map/project/pallas_call | solution.py:1000
  84.7 24.8 %inner.1 = (f32[1024,1536]{1,0:T(8,128)}, f32[1024,1536]{1,0:T(8,128)}, bf16[8,16,1536]{2,1,0:T(8,128)(2,1)}) custom-call(s32[1,5]{1,0:T(1,128)} %pad_add_fusion.info, bf16[1024,768]{1,0:T(8,128)(2,1)} %get-tuple-element.71.normed, bf16[768,3352]{1,0:T(8,128)(2,1)} %bitcast.30, bf16[1024,256]{1,0:T(8,128)(2,1)} %get-tuple-element.72.maps, ...), custom_call_target="tpu_custom_call" | custom-call | tf_op jit(solution)/shard_map/inner/pallas_call | solution.py:1000
  109.5 28.7 %gate.1 = (bf16[1024,768]{1,0:T(8,128)(2,1)}, bf16[1024,1536]{1,0:T(8,128)(2,1)}, bf16[1024,768]{1,0:T(8,128)(2,1)}, bf16[1024,1536]{1,0:T(8,128)(2,1)}, bf16[10...) custom-call(s32[1,5]{1,0:T(1,128)} %pad_add_fusion.info, ...), custom_call_target="tpu_custom_call" | custom-call | tf_op jit(solution)/shard_map/gate/pallas_call | solution.py:1000
  138.2 32.3 %inner_back.1 = (f32[1024,1536]{1,0:T(8,128)}, f32[1024,256]{1,0:T(8,128)}, f32[1024,24]{1,0:T(8,128)}, bf16[1536,768]{1,0:T(8,128)(2,1)}, bf16[768,1536]{1,0:T(8,128)(2,1)}, /*index=5*/bf16[8,16,1536]{2,1,0:T(8,128)(2,1)}) custom-call(s32[1,5]{1,0:T(1,128)} %pad_add_fusion.info, bf16[1024,256]{1,0:T(8,128)(2,1)} %get-tuple-element.72.maps, ...), custom_call_target="tpu_custom_call" | custom-call | tf_op jit(solution)/shard_map/inner_back/pallas_call | solution.py:1000
  170.6 50.3 %finish.1 = (bf16[1024,1816]{1,0:T(8,128)(2,1)}, bf16[16,1816]{1,0:T(8,128)(2,1)}, bf16[1024,768]{1,0:T(8,128)(2,1)}, f32[16,768]{1,0:T(8,128)}, f32[16,768]{1,0...) custom-call(s32[1,5]{1,0:T(1,128)} %pad_add_fusion.info, bf16[1024,768]{1,0:T(8,128)(2,1)} %bitcast.35, ...), custom_call_target="tpu_custom_call" | custom-call | tf_op jit(solution)/shard_map/finish/pallas_call | solution.py:1000
  220.8 37.7 %last.1 = (f32[24,3352]{1,0:T(8,128)}, f32[4,56]{1,0:T(4,128)}, f32[1,56]{1,0:T(1,128)}, f32[1,48]{1,0:T(1,128)}, f32[1,24]{1,0:T(1,128)}, /*index=5*/f32[1,24]{...) custom-call(bf16[1024,768]{1,0:T(8,128)(2,1)} %get-tuple-element.71.normed, ...), custom_call_target="tpu_custom_call" | custom-call | tf_op jit(solution)/shard_map/last/pallas_call | solution.py:1000
  258.6 1.6 slice.11
  260.2 1.2 maximum_bitcast_fusion
  262.0 0.7 copy.35
  262.7 0.6 copy.36
  263.3 0.5 copy.37
  263.8 0.5 copy.38
  265.9 0.7 copy.42
  (26 shorter events, 2.1 us)
Async XLA Ops:
  258.5 1.7 copy-start.2
  258.5 2.9 %copy-start.9 = (f32[1,24]{1,0:T(1,128)S(1)}, f32[1,24]{1,0:T(1,128)}, u32[]{:S(2)}) copy-start(f32[1,24]{1,0:T(1,128)} %get-tuple-element.116) | copy-start | bytes 292
  258.5 3.4 %copy-start = (f32[24,3352]{1,0:T(8,128)S(1)}, f32[24,3352]{1,0:T(8,128)}, u32[]{:S(2)}) copy-start(f32[24,3352]{1,0:T(8,128)} %get-tuple-element.141) | copy-start | bytes 965380
  258.5 4.2 %copy-start.3 = (f32[4,56]{1,0:T(4,128)S(1)}, f32[4,56]{1,0:T(4,128)}, u32[]{:S(2)}) copy-start(f32[4,56]{1,0:T(4,128)} %get-tuple-element.142) | copy-start | bytes 2692
  258.6 4.7 %copy-start.8 = (f32[1,56]{1,0:T(1,128)S(1)}, f32[1,56]{1,0:T(1,128)}, u32[]{:S(2)}) copy-start(f32[1,56]{1,0:T(1,128)} %get-tuple-element.119) | copy-start | bytes 676
  258.6 5.2 %copy-start.7 = (f32[1,24]{1,0:T(1,128)S(1)}, f32[1,24]{1,0:T(1,128)}, u32[]{:S(2)}) copy-start(f32[1,24]{1,0:T(1,128)} %get-tuple-element.120) | copy-start | bytes 292
  258.6 5.7 %copy-start.6 = (f32[1,24]{1,0:T(1,128)S(1)}, f32[1,24]{1,0:T(1,128)}, u32[]{:S(2)}) copy-start(f32[1,24]{1,0:T(1,128)} %get-tuple-element.121) | copy-start | bytes 292
  258.6 6.2 %copy-start.5 = (f32[1,24]{1,0:T(1,128)S(1)}, f32[1,24]{1,0:T(1,128)}, u32[]{:S(2)}) copy-start(f32[1,24]{1,0:T(1,128)} %get-tuple-element.122) | copy-start | bytes 292
  258.6 6.8 %copy-start.4 = (f32[1,48]{1,0:T(1,128)S(1)}, f32[1,48]{1,0:T(1,128)}, u32[]{:S(2)}) copy-start(f32[1,48]{1,0:T(1,128)} %get-tuple-element.123) | copy-start | bytes 580
  258.6 7.3 %copy-start.1 = (f32[48,768]{1,0:T(8,128)S(1)}, f32[48,768]{1,0:T(8,128)}, u32[]{:S(2)}) copy-start(f32[48,768]{1,0:T(8,128)} %get-tuple-element.148) | copy-start | bytes 442372
